TPU v7x, 512 devices: a whole 4x4x16 slice. The times are simulated.
512 devices in a mesh: section: 2 (over core), seq: 32 (over y_lo, z), tensor: 8 (over x, y_hi).
Axes of the slice: x: 4, y: 4 (y_hi: 2, y_lo: 2; y = y_hi * 2 + y_lo), z: 16, core: 2. Of those that a mesh axis runs over, the one named last changes fastest.
Arguments:
- queries: bfloat16 [65536, 4096], P(('section', 'seq'), 'tensor'), may hold values from -18 to 18
- store_kv: bfloat16 [2, 24576, 4096], P(None, ('section', 'seq'), 'tensor'), may hold values from -6 to 6
- out_grad: bfloat16 [65536, 4096], P(('section', 'seq'), 'tensor'), may hold values from -48 to 48
- neighbour_owner: int32 [1024, 2], P(('section', 'seq', 'tensor')), may hold values from 0 to 31, all different within a row; in each aligned block of 16 rows (0 to 15, 16 to 31, ...) at most 2 rows name the same one
- neighbour_slot: int32 [1024, 2], P(('section', 'seq', 'tensor')), may hold values from 0 to 2
- neighbour_count: int32 [1024], P(('section', 'seq', 'tensor')), may hold values from 1 to 2
Outputs:
- attended: bfloat16 [65536, 4096], P(('section', 'seq'), 'tensor')
- store_grad: bfloat16 [2, 24576, 4096], P(None, ('section', 'seq'), 'tensor')
Inputs may be any that keep to these rules, and one draw needn't show every extreme that they name: `neighbour_owner`: each span names 2 different owners. Among the 16 spans of one device (aligned blocks of rows), no owner is named more than 2 times; that many is reached in some blocks.
All inputs are finite; a program needn't handle non-finite values.
Results may differ from a plain program's by a relative error of at most 0.0065.
Values may be sent and summed in bfloat16 or wider, within the bound.
A program may use at most 128 MiB of HBM per device.

v0:
```python
import jax
import jax.numpy as jnp
from jax import lax
from jax.sharding import PartitionSpec as P

HEAD_DIM = 128
SPAN = 64
NLEN = 128
NEIGH = 2


slot_block = 8


def partner(value, axis, distance):
    return lax.ppermute(value, axis, [(i, i ^ 1 << distance) for i in range(lax.axis_size(axis))])


def fetch_rows(meta_block, key_rows, value_rows):
    valid = meta_block >= 0
    safe_meta = jnp.maximum(meta_block, 0)
    keys_out = jnp.take(key_rows, safe_meta, axis=0)
    values_out = jnp.take(value_rows, safe_meta, axis=0)
    return (valid, safe_meta, keys_out, values_out)


def owner_forward(query_in, meta_in, key_rows, value_rows, block_total):
    slot_total, span_len, width = query_in.shape
    heads = width // HEAD_DIM
    neigh_len = key_rows.shape[1]
    scaling = HEAD_DIM ** (-0.5)

    def block_step(index, buffers):
        parts, sums = buffers
        start = index * slot_block
        q_block = lax.dynamic_slice_in_dim(query_in, start, slot_block, 0).reshape(
            slot_block, span_len, heads, HEAD_DIM
        )
        meta_block = lax.dynamic_slice_in_dim(meta_in, start, slot_block, 0)
        valid, safe_meta, k_block, v_block = fetch_rows(meta_block, key_rows, value_rows)
        k_block = k_block.reshape(slot_block, neigh_len, heads, HEAD_DIM)
        v_block = v_block.reshape(slot_block, neigh_len, heads, HEAD_DIM)
        scores = (
            jnp.einsum("sqhd,skhd->shqk", q_block, k_block, preferred_element_type=jnp.float32)
            * scaling
        )
        row_max = jnp.max(scores, axis=-1, keepdims=True)
        local_lse = row_max[..., 0] + jnp.log(jnp.sum(jnp.exp(scores - row_max), axis=-1))
        weights = jnp.exp(scores - local_lse[..., None]).astype(jnp.bfloat16)
        partial_value = jnp.einsum(
            "shqk,skhd->sqhd", weights, v_block, preferred_element_type=jnp.float32
        ).astype(jnp.bfloat16)
        parts = lax.dynamic_update_slice_in_dim(
            parts, partial_value.reshape(slot_block, span_len, width), start, 0
        )
        sums = lax.dynamic_update_slice_in_dim(sums, jnp.transpose(local_lse, (0, 2, 1)), start, 0)
        return (parts, sums)

    init = (jnp.zeros_like(query_in), jnp.zeros((slot_total, span_len, heads), jnp.float32))
    return lax.fori_loop(0, block_total, block_step, init)


def owner_backward(
    query_in, grad_in, total_in, delta_in, meta_in, key_rows, value_rows, block_total
):
    slot_total, span_len, width = query_in.shape
    heads = width // HEAD_DIM
    entry_total, neigh_len = (key_rows.shape[0], key_rows.shape[1])
    scaling = HEAD_DIM ** (-0.5)

    def block_step(index, sums):
        grad_keys, grad_values = sums
        start = index * slot_block
        q_block = lax.dynamic_slice_in_dim(query_in, start, slot_block, 0).reshape(
            slot_block, span_len, heads, HEAD_DIM
        )
        g_block = lax.dynamic_slice_in_dim(grad_in, start, slot_block, 0).reshape(
            slot_block, span_len, heads, HEAD_DIM
        )
        total_block = jnp.transpose(
            lax.dynamic_slice_in_dim(total_in, start, slot_block, 0), (0, 2, 1)
        )
        delta_block = jnp.transpose(
            lax.dynamic_slice_in_dim(delta_in, start, slot_block, 0), (0, 2, 1)
        )
        meta_block = lax.dynamic_slice_in_dim(meta_in, start, slot_block, 0)
        valid, safe_meta, k_block, v_block = fetch_rows(meta_block, key_rows, value_rows)
        k_block = k_block.reshape(slot_block, neigh_len, heads, HEAD_DIM)
        v_block = v_block.reshape(slot_block, neigh_len, heads, HEAD_DIM)
        scores = (
            jnp.einsum("sqhd,skhd->shqk", q_block, k_block, preferred_element_type=jnp.float32)
            * scaling
        )
        prob = jnp.exp(scores - total_block[..., None])
        prob = jnp.where(valid[:, None, None, None], prob, 0.0)
        prob_low = prob.astype(jnp.bfloat16)
        value_grad = jnp.einsum(
            "shqk,sqhd->skhd", prob_low, g_block, preferred_element_type=jnp.float32
        )
        prob_grad = jnp.einsum(
            "sqhd,skhd->shqk", g_block, v_block, preferred_element_type=jnp.float32
        )
        score_grad = (prob * (prob_grad - delta_block[..., None])).astype(jnp.bfloat16)
        key_grad = (
            jnp.einsum("shqk,sqhd->skhd", score_grad, q_block, preferred_element_type=jnp.float32)
            * scaling
        )
        grad_keys = grad_keys.at[safe_meta].add(key_grad.reshape(slot_block, neigh_len, width))
        grad_values = grad_values.at[safe_meta].add(
            value_grad.reshape(slot_block, neigh_len, width)
        )
        return (grad_keys, grad_values)

    init = (
        jnp.zeros((entry_total, neigh_len, width), jnp.float32),
        jnp.zeros((entry_total, neigh_len, width), jnp.float32),
    )
    return lax.fori_loop(0, block_total, block_step, init)


def place_units(unit_rows, slot_dest, slot_total):
    empty = jnp.zeros((slot_total,) + unit_rows.shape[1:], unit_rows.dtype)
    return empty.at[slot_dest].set(unit_rows)


def per_device(queries, store_kv, out_grad, neighbour_owner, neighbour_slot, neighbour_count):
    query_pair, grad_pair, owner_part, slot_part, count_part = partner(
        (queries, out_grad, neighbour_owner, neighbour_slot, neighbour_count), "section", 0
    )
    owners, slots, counts = (
        lax.all_gather(owner_part, "tensor", axis=0, tiled=True),
        lax.all_gather(slot_part, "tensor", axis=0, tiled=True),
        lax.all_gather(count_part, "tensor", axis=0, tiled=True),
    )
    spans = counts.shape[0]
    units = spans * NEIGH
    width = query_pair.shape[1]
    heads = width // HEAD_DIM
    entry_total = store_kv.shape[1] // NLEN
    key_rows = store_kv[0].reshape(entry_total, NLEN, width)
    value_rows = store_kv[1].reshape(entry_total, NLEN, width)
    owner_total = lax.axis_size("seq")
    capacity = max(2, NEIGH * spans // owner_total)
    slot_total = owner_total * capacity
    owner_units = owners.reshape(units)
    slot_units = slots.reshape(units)
    is_live = (jnp.arange(NEIGH)[None, :] < counts[:, None]).reshape(units)
    same_owner = owner_units[:, None] == owner_units[None, :]
    earlier = jnp.arange(units)[None, :] < jnp.arange(units)[:, None]
    slot_rank = jnp.sum((same_owner & earlier).astype(jnp.int32), axis=1)
    slot_dest = owner_units * capacity + slot_rank
    meta_units = jnp.where(is_live, slot_units, -1).astype(jnp.int32)
    meta_buf = jnp.full((slot_total,), -1, jnp.int32).at[slot_dest].set(meta_units)
    query_spans = query_pair.reshape(spans, SPAN, width)
    grad_spans = grad_pair.reshape(spans, SPAN, width)
    query_buf = place_units(jnp.repeat(query_spans, NEIGH, axis=0), slot_dest, slot_total)
    query_in, meta_in = (
        lax.all_to_all(query_buf, "seq", split_axis=0, concat_axis=0, tiled=True),
        lax.all_to_all(meta_buf, "seq", split_axis=0, concat_axis=0, tiled=True),
    )
    block_total = slot_total // slot_block
    parts, local_sums = owner_forward(query_in, meta_in, key_rows, value_rows, block_total)
    parts_back = lax.all_to_all(parts, "seq", split_axis=0, concat_axis=0, tiled=True)
    sums_back = lax.all_to_all(local_sums, "seq", split_axis=0, concat_axis=0, tiled=True)
    part_units = jnp.take(parts_back, slot_dest, axis=0)
    sum_units = jnp.take(sums_back, slot_dest, axis=0)
    sums_four = sum_units.reshape(spans, NEIGH, SPAN, heads)
    live_four = is_live.reshape(spans, NEIGH)[:, :, None, None]
    masked = jnp.where(live_four, sums_four, -1e30)
    row_top = jnp.max(masked, axis=1, keepdims=True)
    lse_total = row_top[:, 0] + jnp.log(
        jnp.sum(jnp.where(live_four, jnp.exp(masked - row_top), 0.0), axis=1)
    )
    mixing = jnp.where(live_four, jnp.exp(masked - lse_total[:, None]), 0.0)
    parts_five = part_units.reshape(spans, NEIGH, SPAN, heads, HEAD_DIM).astype(jnp.float32)
    attended = jnp.sum(mixing[..., None] * parts_five, axis=1)
    attended_low = attended.astype(jnp.bfloat16)
    attended_back = lax.optimization_barrier(attended_low).astype(jnp.float32)
    delta = jnp.sum(
        grad_pair.reshape(spans, SPAN, heads, HEAD_DIM).astype(jnp.float32) * attended_back, axis=-1
    )
    total_buf = place_units(jnp.repeat(lse_total, NEIGH, axis=0), slot_dest, slot_total)
    delta_buf = place_units(jnp.repeat(delta, NEIGH, axis=0), slot_dest, slot_total)
    total_in, delta_in = (
        lax.all_to_all(total_buf, "seq", split_axis=0, concat_axis=0, tiled=True),
        lax.all_to_all(delta_buf, "seq", split_axis=0, concat_axis=0, tiled=True),
    )
    grad_buf = place_units(jnp.repeat(grad_spans, NEIGH, axis=0), slot_dest, slot_total)
    grad_got = lax.all_to_all(grad_buf, "seq", split_axis=0, concat_axis=0, tiled=True)
    grad_keys, grad_values = owner_backward(
        query_in, grad_got, total_in, delta_in, meta_in, key_rows, value_rows, block_total
    )
    store_grad = (
        jnp.stack([grad_keys, grad_values])
        .reshape(2, entry_total * NLEN, width)
        .astype(jnp.bfloat16)
    )
    attended_rows = partner(attended_low.reshape(spans * SPAN, width), "section", 0)
    return (attended_rows, store_grad)


def solution(mesh):
    in_specs = (
        P(("section", "seq"), "tensor"),
        P(None, ("section", "seq"), "tensor"),
        P(("section", "seq"), "tensor"),
        P(("section", "seq", "tensor"), None),
        P(("section", "seq", "tensor"), None),
        P(("section", "seq", "tensor")),
    )
    out_specs = (P(("section", "seq"), "tensor"), P(None, ("section", "seq"), "tensor"))
    return jax.shard_map(
        per_device, mesh=mesh, in_specs=in_specs, out_specs=out_specs, check_vma=False
    )
```

profile of v0, /device:TPU:1, one launch (start us, length us, event | category | flops | bytes accessed | tf_op | source)
XLA Modules:
  0.0 993.0 jit_solution(8915708399058946210)
XLA Ops:
  0.6 8.8 collective-permute-start.3
  17.9 5.4 all-reduce
  23.3 19.4 %all-gather = s32[8,2,2]{2,1,0:T(2,128)S(1)} all-gather(s32[1,2,2]{2,1,0:T(2,128)S(1)} %bitcast.169), channel_id=1, replica_groups=mesh['section'=2,'seq'=32,'tensor'=8] {'tensor'}, dimensions={0}, use_global_device_ids=true | all-gather | bytes 144 | tf_op jit(solution)/shard_map/all_gather | solution.py:131
  42.9 15.8 %all-gather.1 = s32[8,2,2]{2,1,0:T(2,128)S(1)} all-gather(s32[1,2,2]{2,1,0:T(2,128)S(1)} %bitcast.168), channel_id=1, replica_groups=mesh['section'=2,'seq'=32,'tensor'=8] {'tensor'}, dimensions={0}, use_global_device_ids=true | all-gather | bytes 144 | tf_op jit(solution)/shard_map/all_gather | solution.py:132
  60.5 12.9 %all-to-all-start = ((s32[32,2,1]{1,2,0:T(1,128)}), s32[32,2,1]{1,2,0:T(1,128)S(1)}, u32[]{:S(2)}, u32[]{:S(2)}) async-start(s32[32,2,1]{1,2,0:T(1,128)} %bitcast.15), calls=%async_computation | async-start | bytes 32768 | tf_op jit(solution)/shard_map/all_to_all | solution.py:159
  78.3 5.4 scatter_fusion.2
  85.5 11.0 %all-to-all-start.1 = ((bf16[64,64,512]{2,1,0:T(8,128)(2,1)}), bf16[64,64,512]{2,1,0:T(8,128)(2,1)}, u32[]{:S(2)}, u32[]{:S(2)}) async-start(bf16[64,64,512]{2,1,0:T(8,128)(2,1)} %scatter_fusion.2), calls=%async_computation.1 | async-start | bytes 8388608 | tf_op jit(solution)/shard_map/all_to_all | solution.py:158
  97.9 183.1 %all-to-all-done.1 = bf16[64,64,512]{2,1,0:T(8,128)(2,1)} async-done(((bf16[64,64,512]{2,1,0:T(8,128)(2,1)}), bf16[64,64,512]{2,1,0:T(8,128)(2,1)}, u32[]{:S(2)}, u32[]{:S(2)}) %all-to-all-start.1) | async-done | bytes 4194336 | tf_op jit(solution)/shard_map/all_to_all | solution.py:158
  283.6 45.1 %while.30 = (s32[]{:T(128)}, bf16[64,64,512]{2,1,0:T(8,128)(2,1)}, f32[64,64,4]{1,2,0:T(4,128)S(1)}, s32[64]{0:T(128)S(1)}, bf16[3,128,512]{2,1,0:T(8,128)(2,1)S...) while((s32[]{:T(128)}, bf16[64,64,512]{2,1,0:T(8,128)(2,1)}, ...), condition=%wide.region_6.8_spmd, body=%wide.region_3.7_spmd.sunk | while | flops 137100320 | bytes 15831387 | solution.py:60
  328.8 19.6 %all_to_all.42 = f32[32,1,512]{2,1,0:T(1,128)S(1)} all-to-all(f32[32,1,512]{2,1,0:T(1,128)S(1)} %reshape.367), channel_id=1, replica_groups=mesh['section'=2,'seq'=32,'tensor'=8] {'seq'}, dimensions={0} | all-to-all | bytes 131072 | tf_op jit(solution)/shard_map/all_to_all | solution.py:164
  348.4 4.9 all-to-all-start.3
  353.3 6.7 collective-permute-start.5
  370.5 165.8 %all-to-all-done.3 = bf16[64,64,512]{2,1,0:T(8,128)(2,1)} async-done(((bf16[64,64,512]{2,1,0:T(8,128)(2,1)}), bf16[64,64,512]{2,1,0:T(8,128)(2,1)}, u32[]{:S(2)}, u32[]{:S(2)}) %all-to-all-start.3) | async-done | bytes 4194336 | tf_op jit(solution)/shard_map/all_to_all | solution.py:163
  536.2 10.9 %all-to-all-start.4 = ((f32[32,1,512]{2,1,0:T(1,128)}), f32[32,1,512]{2,1,0:T(1,128)S(1)}, u32[]{:S(2)}, u32[]{:S(2)}) async-start(f32[32,1,512]{2,1,0:T(1,128)} %reshape.369), calls=%async_computation.4 | async-start | bytes 131072 | tf_op jit(solution)/shard_map/all_to_all | solution.py:185
  552.1 4.9 multiply_reduce_fusion
  562.7 12.4 %all-to-all-start.6 = ((f32[32,1,512]{2,1,0:T(1,128)}), f32[32,1,512]{2,1,0:T(1,128)S(1)}, u32[]{:S(2)}, u32[]{:S(2)}) async-start(f32[32,1,512]{2,1,0:T(1,128)} %reshape.371), calls=%async_computation.6 | async-start | bytes 131072 | tf_op jit(solution)/shard_map/all_to_all | solution.py:186
  579.2 6.3 scatter_fusion.4
  588.4 9.7 all-to-all-start.5
  605.9 176.4 %all-to-all-done.5 = bf16[64,64,512]{2,1,0:T(8,128)(2,1)} async-done(((bf16[64,64,512]{2,1,0:T(8,128)(2,1)}), bf16[64,64,512]{2,1,0:T(8,128)(2,1)}, u32[]{:S(2)}, u32[]{:S(2)}) %all-to-all-start.5) | async-done | bytes 4194336 | tf_op jit(solution)/shard_map/all_to_all | solution.py:189
  784.3 203.1 %while.31 = (s32[]{:T(128)}, f32[3,128,512]{2,1,0:T(8,128)}, f32[3,128,512]{2,1,0:T(8,128)}, s32[64]{0:T(128)S(1)}, bf16[64,64,512]{2,1,0:T(8,128)(2,1)}, /*inde...) while((s32[]{:T(128)}, f32[3,128,512]{2,1,0:T(8,128)}, ...), condition=%wide.region_17.19_spmd, body=%wide.region_14.18_spmd.sunk | while | flops 272892960 | bytes 49339296 | solution.py:118
  845.5 4.6 scatter_fusion.1
  896.3 4.5 scatter_fusion.1
  946.9 4.6 scatter_fusion.1
  972.5 4.5 scatter_fusion.1
  (389 shorter events, 292.4 us)
Async XLA Ops:
  0.6 72.8 %collective-permute-start.3 = (bf16[1024,512]{1,0:T(8,128)(2,1)}, bf16[1024,512]{1,0:T(8,128)(2,1)S(1)}, u32[]{:S(2)}, u32[]{:S(2)}) collective-permute-start(bf16[1024,512]{1,0:T(8,128)(2,1)} %param.12), channel_id=1, source_target_pairs={{0,256},{256,0},{1,257},{257,1},{2,258},{258,2},{3,259},{259,3},{4... | collective-permute-start | bytes 3145736 | tf_op jit(solution)/shard_map/ppermute | solution.py:16
  9.4 13.9 %collective-permute-start.1 = (s32[2,2]{1,0:T(2,128)}, s32[2,2]{1,0:T(2,128)S(1)}, u32[]{:S(2)}, u32[]{:S(2)}) collective-permute-start(s32[2,2]{1,0:T(2,128)} %param.15), channel_id=1, source_target_pairs={{0,256},{256,0},{1,257},{257,1},{2,258},{258,2},{3,259},{259,3},{4... | collective-permute-start | bytes 56 | tf_op jit(solution)/shard_map/ppermute | solution.py:16
  11.4 6.3 collective-permute-start
  13.8 29.1 %collective-permute-start.2 = (s32[2,2]{1,0:T(2,128)}, s32[2,2]{1,0:T(2,128)S(1)}, u32[]{:S(2)}, u32[]{:S(2)}) collective-permute-start(s32[2,2]{1,0:T(2,128)} %param.16), channel_id=1, source_target_pairs={{0,256},{256,0},{1,257},{257,1},{2,258},{258,2},{3,259},{259,3},{4... | collective-permute-start | bytes 56 | tf_op jit(solution)/shard_map/ppermute | solution.py:16
  60.5 25.0 %all-to-all-start = ((s32[32,2,1]{1,2,0:T(1,128)}), s32[32,2,1]{1,2,0:T(1,128)S(1)}, u32[]{:S(2)}, u32[]{:S(2)}) async-start(s32[32,2,1]{1,2,0:T(1,128)} %bitcast.15), calls=%async_computation | async-start | bytes 32768 | tf_op jit(solution)/shard_map/all_to_all | solution.py:159
  83.8 12.8 %copy-start.6 = (bf16[2,384,512]{2,1,0:T(8,128)(2,1)S(1)}, bf16[2,384,512]{2,1,0:T(8,128)(2,1)}, u32[]{:S(2)}) copy-start(bf16[2,384,512]{2,1,0:T(8,128)(2,1)} %param.13) | copy-start | bytes 2359300
  85.5 195.5 %all-to-all-start.1 = ((bf16[64,64,512]{2,1,0:T(8,128)(2,1)}), bf16[64,64,512]{2,1,0:T(8,128)(2,1)}, u32[]{:S(2)}, u32[]{:S(2)}) async-start(bf16[64,64,512]{2,1,0:T(8,128)(2,1)} %scatter_fusion.2), calls=%async_computation.1 | async-start | bytes 8388608 | tf_op jit(solution)/shard_map/all_to_all | solution.py:158
  348.4 187.8 %all-to-all-start.3 = ((bf16[64,64,512]{2,1,0:T(8,128)(2,1)}), bf16[64,64,512]{2,1,0:T(8,128)(2,1)}, u32[]{:S(2)}, u32[]{:S(2)}) async-start(bf16[64,64,512]{2,1,0:T(8,128)(2,1)} %get-tuple-element.299), calls=%async_computation.3 | async-start | bytes 8388608 | tf_op jit(solution)/shard_map/all_to_all | solution.py:163
  353.3 9.2 collective-permute-start.5
  536.2 26.5 %all-to-all-start.4 = ((f32[32,1,512]{2,1,0:T(1,128)}), f32[32,1,512]{2,1,0:T(1,128)S(1)}, u32[]{:S(2)}, u32[]{:S(2)}) async-start(f32[32,1,512]{2,1,0:T(1,128)} %reshape.369), calls=%async_computation.4 | async-start | bytes 131072 | tf_op jit(solution)/shard_map/all_to_all | solution.py:185
  552.1 5.0 copy-start.2
  559.1 16.1 %copy-start.4 = (bf16[1024,512]{1,0:T(8,128)(2,1)S(1)}, bf16[1024,512]{1,0:T(8,128)(2,1)}, u32[]{:S(2)}) copy-start(bf16[1024,512]{1,0:T(8,128)(2,1)} %copy-done.3) | copy-start | bytes 3145732
  562.7 25.7 %all-to-all-start.6 = ((f32[32,1,512]{2,1,0:T(1,128)}), f32[32,1,512]{2,1,0:T(1,128)S(1)}, u32[]{:S(2)}, u32[]{:S(2)}) async-start(f32[32,1,512]{2,1,0:T(1,128)} %reshape.371), calls=%async_computation.6 | async-start | bytes 131072 | tf_op jit(solution)/shard_map/all_to_all | solution.py:186
  588.4 193.9 %all-to-all-start.5 = ((bf16[64,64,512]{2,1,0:T(8,128)(2,1)}), bf16[64,64,512]{2,1,0:T(8,128)(2,1)}, u32[]{:S(2)}, u32[]{:S(2)}) async-start(bf16[64,64,512]{2,1,0:T(8,128)(2,1)} %scatter_fusion.4), calls=%async_computation.5 | async-start | bytes 8388608 | tf_op jit(solution)/shard_map/all_to_all | solution.py:189
  600.3 390.5 %collective-permute-start.4 = (bf16[1024,512]{1,0:T(8,128)(2,1)}, bf16[1024,512]{1,0:T(8,128)(2,1)}, u32[]{:S(2)}, u32[]{:S(2)}) collective-permute-start(bf16[1024,512]{1,0:T(8,128)(2,1)} %bitcast.101), channel_id=1, source_target_pairs={{0,256},{256,0},{1,257},{257,1},{2,258},{258,2},{3,259},{259,3},{4... | collective-permute-start | bytes 3145736 | tf_op jit(solution)/shard_map/ppermute | solution.py:16
  805.4 4.2 copy-start.10
  830.6 4.4 copy-start.10
  856.2 4.4 copy-start.10
  865.5 3.6 copy-start.1
  881.6 4.3 copy-start.10
  907.0 4.2 copy-start.10
  932.2 4.3 copy-start.10
  957.7 4.4 copy-start.10
  983.2 4.2 copy-start.10
  (49 other events, 99.4 us)
where the time goes:
time: 1000 us; the launch traced here: 993 us
  waiting for transfers between devices  532 us (53%)
  local copies, waits for them, and re-layouts  128 us (13%)
  other arithmetic  107 us (11%)
  starting transfers between devices  87.5 us (9%)
  matrix products  75.3 us (8%)
  blocking collectives  60.2 us (6%)
    all_to_all x1, waiting for transfers between devices, per_device(): lax.all_to_all(query_buf, 'seq', split_axis=0, concat_axis=0, tiled=True)  183 us
    all_to_all x1, waiting for transfers between devices, per_device(): lax.all_to_all(grad_buf, 'seq', split_axis=0, concat_axis=0, tiled=True)  176 us
    all_to_all x1, waiting for transfers between devices, per_device(): lax.all_to_all(parts, 'seq', split_axis=0, concat_axis=0, tiled=True)  166 us
    scatter-add x8, other arithmetic, block_step(): grad_values.at[safe_meta]  36 us
    scatter-add x8, other arithmetic, block_step(): grad_keys.at[safe_meta].add(key_grad.reshape(slot_block, neigh_len, width))  34.2 us
    dot_general x8, matrix products, block_step(): jnp.einsum('shqk,sqhd->skhd', score_grad, q_block, preferred_element_type...  33.8 us
    ppermute x6, starting transfers between devices, partner(): lax.ppermute(value, axis, [(i, i ^ 1 << distance) for i in range(lax.axis...  25.7 us
    dot_general x16, matrix products, block_step(): jnp.einsum('sqhd,skhd->shqk', q_block, k_block, preferred_element_type=jn...  22.4 us
  transfers between devices with their start and end apart: 12, of which 6 were waited for; matrix products, arithmetic and copies ran while one was open for 26% of the time, Pallas kernels for 0%

commit v1 on v0

v1 whole, which is shorter than its diff:
```python
import functools

import jax
import jax.numpy as jnp
from jax import lax
from jax.experimental import pallas as pl
from jax.experimental.pallas import tpu as pltpu
from jax.sharding import PartitionSpec as P

HEAD_DIM = 128
SPAN = 64
NLEN = 128
NEIGH = 2
SLOTS = 4
MESH = pl.DeviceIdType.MESH
DEAD = -1e30
NONE = -100000


def kernel(nz, ch, heads, tab, q_in, kv_in, g_in, att_out, sg_out,
           kv, q_own, q_nbr, g_own, g_nbr, pb, dpb, rs, fin, asend, arecv, att,
           lse, gp, st_s, st_r, wts, dlt,
           ag_s, ag_r, loc_s, loc_r, qg_s, qg_r, own_l, stx_s, stx_r,
           rs_s, rs_r, a_s, a_r, f_s, f_r, o_l):
    half = nz // 2
    stride = 2 * ch
    slots = nz * SLOTS
    scaling = HEAD_DIM ** (-0.5)
    q_blk, g_blk = (q_own, q_nbr), (g_own, g_nbr)
    sec = lax.axis_index("section")
    seq = lax.axis_index("seq")
    y, z = lax.div(seq, nz), lax.rem(seq, nz)
    up, down = lax.rem(z + 1, nz), lax.rem(z + nz - 1, nz)
    z_to = (up, down)

    def dev(s, yy, zz):
        return {"section": s, "seq": yy * nz + zz}

    sibling = dev(1 - sec, y, z)
    y_nbr = dev(sec, 1 - y, z)

    def remote(src, dst, ssem, rsem, device):
        return pltpu.make_async_remote_copy(
            src_ref=src, dst_ref=dst, send_sem=ssem, recv_sem=rsem,
            device_id=device, device_id_type=MESH)

    barrier = pltpu.get_barrier_semaphore()
    for device in (sibling, y_nbr, dev(sec, y, up), dev(sec, y, down),
                   dev(1 - sec, y, up), dev(1 - sec, y, down)):
        pl.semaphore_signal(barrier, inc=1, device_id=device, device_id_type=MESH)
    own_q = pltpu.make_async_copy(q_in, q_own, own_l.at[0])
    own_g = pltpu.make_async_copy(g_in, g_own, own_l.at[1])
    own_q.start()
    own_g.start()
    pl.semaphore_wait(barrier, 6)

    def place(d, k):
        return nz - k if d == 0 else k

    def first(d, c):
        return remote(kv_in.at[c], kv.at[c, place(d, 1)], ag_s.at[d, c, 1], ag_r.at[d, c, 1],
                      dev(1 - sec, y, z_to[d]))

    def forward(d, c, k):
        return remote(kv.at[c, place(d, k - 1)], kv.at[c, place(d, k)], ag_s.at[d, c, k],
                      ag_r.at[d, c, k], dev(sec, y, z_to[d]))

    def arrived(d, c, k):
        here = kv.at[c, place(d, k)]
        remote(here, here, ag_s.at[d, c, k], ag_r.at[d, c, k], dev(sec, y, z_to[d])).wait_recv()

    first(0, 0).start()
    first(1, 1).start()
    first(0, 1).start()
    first(1, 0).start()
    locals_ = [remote(kv_in.at[c], kv.at[c, 0], loc_s.at[c], loc_r.at[c], sibling) for c in (0, 1)]
    for copy in locals_:
        copy.start()
    swap = [remote(q_in, q_nbr, qg_s.at[0], qg_r.at[0], y_nbr),
            remote(g_in, g_nbr, qg_s.at[1], qg_r.at[1], y_nbr)]
    for copy in swap:
        copy.start()

    lse[...] = jnp.full_like(lse, DEAD)
    gp[...] = jnp.zeros_like(gp)
    for d, c, m in ((0, 0, half), (1, 1, half), (0, 1, half - 1), (1, 0, half - 1)):
        rs[d, c, m] = jnp.zeros(rs.shape[3:], rs.dtype)
    lanes = lax.broadcasted_iota(jnp.int32, (SPAN, 128), 1)

    def pick(three, es):
        return jnp.where(es == 0, three[0], jnp.where(es == 1, three[1], three[2]))

    def fwd_item(n, b):
        idx = jnp.where(lax.rem(n, 2) == 1, nz - lax.div(n + 1, 2), lax.div(n, 2))
        for r in (0, 1):
            sl = idx * SLOTS + (b * 2 + r)
            sp, es = tab[sl], tab[slots + sl]
            l_of = (tab[2 * slots + sl], tab[3 * slots + sl])
            stat_l, stat_g = [], []
            for h in range(heads):
                hs = pl.ds(h * HEAD_DIM, HEAD_DIM)
                qv = q_blk[b][sp, :, hs]
                gv = g_blk[b][sp, :, hs]
                ks = pick([kv[0, idx, e, :, hs] for e in range(3)], es)
                vs = pick([kv[1, idx, e, :, hs] for e in range(3)], es)
                s = lax.dot_general(qv, ks, (((1,), (1,)), ((), ())),
                                    preferred_element_type=jnp.float32) * scaling
                dp = lax.dot_general(gv, vs, (((1,), (1,)), ((), ())),
                                     preferred_element_type=jnp.float32)
                top = jnp.max(s, axis=1, keepdims=True)
                p = jnp.exp(s - top)
                tot = jnp.sum(p, axis=1, keepdims=True)
                p = p * (1.0 / tot)
                pb[sl, :, hs] = p
                dpb[sl, :, hs] = dp
                stat_l.append(top + jnp.log(tot))
                stat_g.append(jnp.sum(p * dp, axis=1, keepdims=True))
            for j in range(NEIGH):
                a, g2 = lse[j], gp[j]
                for h in range(heads):
                    hit = lanes == l_of[j] + h * stride
                    a = jnp.where(hit, stat_l[h], a)
                    g2 = jnp.where(hit, stat_g[h], g2)
                lse[j] = a
                gp[j] = g2

    def items(lo, hi, b):
        lax.fori_loop(lo, hi, lambda n, t: (fwd_item(n, b), t)[1], 0)

    own_q.wait()
    own_g.wait()
    for copy in locals_:
        copy.wait_recv()
    lag = min(4, half)

    def nbr_done(k):
        return jnp.minimum(jnp.maximum((k + 1 - lag) * 4, 0), 2 * half - 3)

    def gather_step(k, t):
        for d, c in ((0, 0), (1, 1)):
            arrived(d, c, k)
            forward(d, c, k + 1).start()
        items(jnp.maximum(2 * k - 3, 0), 2 * k - 1, 0)
        for d, c in ((0, 1), (1, 0)):
            arrived(d, c, k)

            @pl.when(k + 1 < half)
            def _():
                forward(d, c, k + 1).start()

        @pl.when(k == lag)
        def _():
            for copy in swap:
                copy.wait_recv()

        items(nbr_done(k - 1), nbr_done(k), 1)
        return t

    lax.fori_loop(1, half, gather_step, 0)
    if half <= lag:
        for copy in swap:
            copy.wait_recv()
    items(2 * half - 3, 2 * half - 1, 0)
    items(nbr_done(half - 1), 2 * half - 1, 1)
    arrived(0, 0, half)
    arrived(1, 1, half)
    fwd_item(2 * half - 1, 0)
    fwd_item(2 * half - 1, 1)

    a0, a1 = lse[0], lse[1]
    top = jnp.maximum(a0, a1)
    lc = top + jnp.log(jnp.exp(a0 - top) + jnp.exp(a1 - top))
    gc = jnp.exp(a0 - lc) * gp[0] + jnp.exp(a1 - lc) * gp[1]
    st_s[0] = lc
    st_s[1] = gc
    stats = remote(st_s, st_r, stx_s.at[0], stx_r.at[0], y_nbr)
    stats.start()
    stats.wait_recv()
    lo_, go_ = st_r[0], st_r[1]
    top = jnp.maximum(lc, lo_)
    total = top + jnp.log(jnp.exp(lc - top) + jnp.exp(lo_ - top))
    dlt[...] = jnp.exp(lc - total) * gc + jnp.exp(lo_ - total) * go_
    wts[0] = jnp.exp(a0 - total)
    wts[1] = jnp.exp(a1 - total)

    def column(values, lane):
        return jnp.sum(jnp.where(lanes == lane, values, 0.0), axis=1, keepdims=True)

    def contribution(c, idx, h):
        hs = pl.ds(h * HEAD_DIM, HEAD_DIM)
        left, right = [], []
        for slot in range(SLOTS):
            b = slot // 2
            sl = idx * SLOTS + slot
            sp, es = tab[sl], tab[slots + sl]
            l0 = tab[2 * slots + sl] + h * stride
            l1 = tab[3 * slots + sl] + h * stride
            w = jnp.where(lanes == l0, wts[0], 0.0) + jnp.where(lanes == l1, wts[1], 0.0)
            p = pb[sl, :, hs] * jnp.sum(w, axis=1, keepdims=True)
            if c == 0:
                p = p * (dpb[sl, :, hs] - column(dlt[...], jnp.maximum(l0, l1)))
                right.append(q_blk[b][sp, :, hs])
            else:
                right.append(g_blk[b][sp, :, hs])
            x = p.astype(jnp.bfloat16)
            zero = jnp.zeros_like(x)
            left.append(jnp.concatenate([jnp.where(es == e, x, zero) for e in range(3)], axis=1))
        out = lax.dot_general(jnp.concatenate(left, axis=0), jnp.concatenate(right, axis=0),
                              (((0,), (0,)), ((), ())), preferred_element_type=jnp.float32)
        if c == 0:
            out = out * scaling
        return out.reshape(3, NLEN, HEAD_DIM)

    def step_on(d, c, m):
        zz = lax.rem(z + 1 + d * (nz - 2), nz)
        return remote(rs.at[d, c, m], rs.at[d, c, m - 1], rs_s.at[d, c, m - 1],
                      rs_r.at[d, c, m - 1], dev(sec, y, zz))

    def sum_arrived(d, c, m):
        here = rs.at[d, c, m]
        remote(here, here, rs_s.at[d, c, m], rs_r.at[d, c, m], y_nbr).wait_recv()

    def chunk(d, c, m):
        idx = jnp.where(d == 0, m, nz - m)
        for h in range(heads):
            hs = pl.ds(h * HEAD_DIM, HEAD_DIM)
            o = contribution(c, idx, h) + rs[d, c, m, :, :, hs].astype(jnp.float32)
            rs[d, c, m, :, :, hs] = o.astype(jnp.bfloat16)
        step_on(d, c, m).start()

    def attended_span(b, sp):
        y_b = y if b == 0 else 1 - y
        outs = []
        for h in range(heads):
            hs = pl.ds(h * HEAD_DIM, HEAD_DIM)
            acc = jnp.zeros((SPAN, HEAD_DIM), jnp.float32)
            for j in range(NEIGH):
                at = 4 * slots + (b * ch + sp) * NEIGH + j
                sl = tab[at]
                idx = tab[at + 2 * ch * NEIGH]
                es = tab[at + 4 * ch * NEIGH]
                w = column(wts[j], y_b * ch + sp + h * stride)
                p = (pb[sl, :, hs] * w).astype(jnp.bfloat16)
                acc += jnp.dot(p, kv[1, idx, es, :, hs], preferred_element_type=jnp.float32)
            outs.append((hs, acc))
        return outs

    def nbr_span(sp, t):
        for hs, acc in attended_span(1, sp):
            asend[sp, :, hs] = acc.astype(jnp.bfloat16)
        return t

    def own_span(sp, t):
        for hs, acc in attended_span(0, sp):
            both = acc + arecv[sp, :, hs].astype(jnp.float32)
            att[sp, :, hs] = both.astype(jnp.bfloat16)
        return t

    give = remote(asend, arecv, a_s.at[0], a_r.at[0], y_nbr)
    events = 2 * half - 1
    per = -(-ch // 4)

    def sum_step(e, t):
        odd = lax.rem(e, 2)
        m = half - lax.div(e + 1, 2)
        for c in (0, 1):
            d = odd if c == 0 else 1 - odd

            @pl.when(e >= 2)
            def _():
                sum_arrived(d, c, m)

            chunk(d, c, m)
        if events >= 15:
            @pl.when(jnp.logical_and(e >= 1, e <= 4))
            def _():
                lax.fori_loop((e - 1) * per, e * per, nbr_span, 0)

            @pl.when(e == 4)
            def _():
                give.start()

            @pl.when(e == 9)
            def _():
                give.wait_recv()

            @pl.when(jnp.logical_and(e >= 9, e <= 12))
            def _():
                lax.fori_loop((e - 9) * per, (e - 8) * per, own_span, 0)
        return t

    lax.fori_loop(0, events, sum_step, 0)
    if events < 15:
        lax.fori_loop(0, ch, nbr_span, 0)
        give.start()
        give.wait_recv()
        lax.fori_loop(0, ch, own_span, 0)
    out_copy = pltpu.make_async_copy(att, att_out, o_l.at[0])
    out_copy.start()
    finals = []
    for c in (1, 0):
        sum_arrived(0, c, 0)
        sum_arrived(1, c, 0)
        for h in range(heads):
            hs = pl.ds(h * HEAD_DIM, HEAD_DIM)
            o = contribution(c, 0, h) + (rs[0, c, 0, :, :, hs].astype(jnp.float32)
                                         + rs[1, c, 0, :, :, hs].astype(jnp.float32))
            fin[c, :, :, hs] = o.astype(jnp.bfloat16)
        copy = remote(fin.at[c], sg_out.at[c], f_s.at[c], f_r.at[c], sibling)
        copy.start()
        finals.append(copy)

    for d, c in ((0, 0), (1, 1), (0, 1), (1, 0)):
        first(d, c).wait_send()
        steps = half + 1 if d == c else half
        lax.fori_loop(2, steps, lambda k, t: (forward(d, c, k).wait_send(), t)[1], 0)
        lax.fori_loop(1, steps, lambda m, t: (step_on(d, c, m).wait_send(), t)[1], 0)
    for copy in locals_ + swap + [stats, give]:
        copy.wait_send()
    for copy in finals:
        copy.wait_send()
        copy.wait_recv()
    out_copy.wait()


def tables(owner_part, slot_part, count_part, nz):
    packed = jnp.concatenate([owner_part, slot_part, count_part[:, None]], axis=1)
    own = lax.all_gather(packed, "tensor", axis=0, tiled=True)
    size = 2 * nz
    other = lax.ppermute(own, "seq", [(i, (i + nz) % size) for i in range(size)])
    meta = jnp.stack([own, other])
    ch = own.shape[0]
    seq = lax.axis_index("seq")
    y, z = seq // nz, seq % nz
    owner, entry, count = meta[..., 0:2], meta[..., 2:4], meta[..., 4:5]
    j_of = jnp.broadcast_to(jnp.arange(NEIGH)[None, None, :], owner.shape)
    used = (j_of < count) & (owner // nz == y)
    units = ch * NEIGH
    shape = owner.shape
    flat = lambda a: jnp.broadcast_to(a, shape).reshape(2, units)
    owner, entry, used, j_of = flat(owner), flat(entry), flat(used), flat(j_of)
    span = flat(jnp.arange(ch)[None, :, None])
    same = (owner[:, :, None] == owner[:, None, :]) & used[:, None, :]
    earlier = jnp.arange(units)[None, :] < jnp.arange(units)[:, None]
    rank = jnp.sum((same & earlier).astype(jnp.int32), axis=2)
    rel = (owner - z) % nz
    block = jnp.arange(2)[:, None]
    dest = rel * SLOTS + block * 2 + rank
    y_b = jnp.where(block == 0, y, 1 - y)
    lane = y_b * ch + span
    slots = nz * SLOTS
    match = ((dest[None] == jnp.arange(slots)[:, None, None]) & used[None]).astype(jnp.int32)
    total = lambda a: jnp.sum(match * a, axis=(1, 2))
    lane_of = [total((lane - NONE) * (j_of == j)) + NONE for j in range(NEIGH)]
    dest = jnp.where(used, dest, 0)
    parts = [total(span), total(entry), lane_of[0], lane_of[1],
             dest.reshape(-1), (dest // SLOTS).reshape(-1), jnp.where(used, entry, 0).reshape(-1)]
    return jnp.concatenate(parts).astype(jnp.int32)


def per_device(nz, queries, store_kv, out_grad, neighbour_owner, neighbour_slot, neighbour_count):
    rows, width = queries.shape
    heads = width // HEAD_DIM
    ch = rows // SPAN
    half = nz // 2
    entries = store_kv.shape[1] // NLEN
    tab = tables(neighbour_owner, neighbour_slot, neighbour_count, nz)
    bf, f32 = jnp.bfloat16, jnp.float32
    dma = pltpu.SemaphoreType.DMA
    block = (entries, NLEN, width)
    spans = (ch, SPAN, width)
    any_spec = pl.BlockSpec(memory_space=pl.ANY)
    attended, store_grad = pl.pallas_call(
        functools.partial(kernel, nz, ch, heads),
        out_shape=[jax.ShapeDtypeStruct(spans, bf), jax.ShapeDtypeStruct((2,) + block, bf)],
        in_specs=[pl.BlockSpec(memory_space=pltpu.SMEM), any_spec, any_spec, any_spec],
        out_specs=[any_spec, any_spec],
        scratch_shapes=[
            pltpu.VMEM((2, nz) + block, bf),
            pltpu.VMEM(spans, bf), pltpu.VMEM(spans, bf),
            pltpu.VMEM(spans, bf), pltpu.VMEM(spans, bf),
            pltpu.VMEM((nz * SLOTS, SPAN, width), f32),
            pltpu.VMEM((nz * SLOTS, SPAN, width), f32),
            pltpu.VMEM((2, 2, half + 1) + block, bf),
            pltpu.VMEM((2,) + block, bf),
            pltpu.VMEM(spans, bf), pltpu.VMEM(spans, bf), pltpu.VMEM(spans, bf),
            pltpu.VMEM((2, SPAN, 128), f32), pltpu.VMEM((2, SPAN, 128), f32),
            pltpu.VMEM((2, SPAN, 128), f32), pltpu.VMEM((2, SPAN, 128), f32),
            pltpu.VMEM((2, SPAN, 128), f32), pltpu.VMEM((SPAN, 128), f32),
            dma((2, 2, half + 1)), dma((2, 2, half + 1)), dma((2,)), dma((2,)),
            dma((2,)), dma((2,)), dma((2,)), dma((1,)), dma((1,)),
            dma((2, 2, half + 1)), dma((2, 2, half + 1)), dma((1,)), dma((1,)),
            dma((2,)), dma((2,)), dma((1,)),
        ],
        compiler_params=pltpu.CompilerParams(
            collective_id=0, has_side_effects=True, vmem_limit_bytes=60 * 1024 * 1024),
        cost_estimate=pl.CostEstimate(flops=4 * 10 ** 9, bytes_accessed=6 * 10 ** 6,
                                      transcendentals=4 * 10 ** 6),
    )(tab, queries.reshape(spans), store_kv.reshape((2,) + block), out_grad.reshape(spans))
    return attended.reshape(rows, width), store_grad.reshape(store_kv.shape)


def solution(mesh):
    nz = mesh.shape["seq"] // 2
    in_specs = (
        P(("section", "seq"), "tensor"),
        P(None, ("section", "seq"), "tensor"),
        P(("section", "seq"), "tensor"),
        P(("section", "seq", "tensor"), None),
        P(("section", "seq", "tensor"), None),
        P(("section", "seq", "tensor")),
    )
    out_specs = (P(("section", "seq"), "tensor"), P(None, ("section", "seq"), "tensor"))
    return jax.shard_map(
        functools.partial(per_device, nz), mesh=mesh, in_specs=in_specs, out_specs=out_specs,
        check_vma=False)
```

time: 1000 us -> 314 us (0.31)
  waiting for transfers between devices: 532 us -> 1.39 us
  Pallas kernels: 0 us -> 282 us
  local copies, waits for them, and re-layouts: 128 us -> 6.85 us
  other arithmetic: 107 us -> 0.63 us
  starting transfers between devices: 87.5 us -> 2.29 us
  matrix products: 75.3 us -> 0 us
  blocking collectives: 60.2 us -> 20.5 us
    all_to_all x6 -> x0, waiting for transfers between devices: 530 us -> none  [the longest x1 183 us: per_device(): lax.all_to_all(query_buf, 'seq', split_axis=0, concat_axis=0, tiled=True)]
    pallas_call x0 -> x1, Pallas kernels: none -> 282 us  [per_device(): pl.pallas_call(functools.partial(kernel, nz, ch, heads), out_shape=[jax.S...]
    dot_general x40 -> x0, matrix products: 75.3 us -> none  [the longest x8 33.8 us: block_step(): jnp.einsum('shqk,sqhd->skhd', score_grad, q_block, preferred_element_type...]
    scatter-add x16 -> x0, other arithmetic: 70.1 us -> none  [the longest x8 36 us: block_step(): grad_values.at[safe_meta]]
    all_to_all x6 -> x0, starting transfers between devices: 61.8 us -> none  [the longest x1 12.9 us: per_device(): lax.all_to_all(meta_buf, 'seq', split_axis=0, concat_axis=0, tiled=True)]
    reshape x17 -> x3, local copies, waits for them, and re-layouts: 30.8 us -> 0.31 us  [tables(): flat = lambda a: jnp.broadcast_to(a, shape).reshape(2, units)]
    gather x35 -> x0, local copies, waits for them, and re-layouts: 25.2 us -> none  [the longest x16 9.83 us: fetch_rows(): keys_out = jnp.take(key_rows, safe_meta, axis=0)]
    ppermute x6 -> x1, starting transfers between devices: 25.7 us -> 2.29 us  [tables(): lax.ppermute(own, 'seq', [(i, (i + nz) % size) for i in range(size)])]
  transfers between devices with their start and end apart: 12 -> 1, of which waited for: 6 -> 1; matrix products, arithmetic and copies ran while one was open for 26% -> 0% of each run, Pallas kernels for 0% -> 0%
where the time goes in v1:
time: 314 us
  Pallas kernels  282 us (90%)
  blocking collectives  20.5 us (7%)
  local copies, waits for them, and re-layouts  6.85 us (2%)
    pallas_call x1, Pallas kernels, per_device(): pl.pallas_call(functools.partial(kernel, nz, ch, heads), out_shape=[jax.S...  282 us
    all_gather x1, blocking collectives, tables(): own = lax.all_gather(packed, 'tensor', axis=0, tiled=True)  20.5 us
  transfers between devices with their start and end apart: 1, of which 1 were waited for; matrix products, arithmetic and copies ran while one was open for 0% of the time, Pallas kernels for 0%

profile of v1, /device:TPU:1, one launch (start us, length us, event | category | flops | bytes accessed | tf_op | source)
XLA Modules:
  0.0 314.2 jit_solution(6887350498737219639)
XLA Ops:
  0.7 0.6 copy-done.3
  1.3 0.1 copy.24
  1.4 0.6 copy-done.1
  2.0 20.5 %all-gather = s32[8,2,5]{2,1,0:T(2,128)S(1)} all-gather(s32[1,2,5]{2,1,0:T(2,128)S(1)} %add_bitcast_fusion), channel_id=1, replica_groups=mesh['section'=2,'seq'=32,'tensor'=8] {'tensor'}, dimensions={0}, use_global_device_ids=true | all-gather | bytes 360 | tf_op jit(solution)/shard_map/all_gather | solution.py:328
  22.6 2.3 collective-permute-start
  25.0 0.1 eq.73
  25.1 0.1 eq.77
  25.6 1.4 collective-permute-done
  27.1 0.1 copy.29
  27.2 0.1 and.74
  27.3 0.1 reshape.189
  27.4 0.1 copy.30
  27.5 0.1 reshape.190
  27.6 0.1 mul.79
  27.7 0.1 copy.28
  27.8 0.1 reshape.188
  27.9 0.2 convert_reduce_fusion
  28.2 0.1 copy.32
  28.3 0.1 sub.50
  28.4 0.1 select_reduce_fusion
  28.6 0.7 concatenate.7.tab
  29.3 281.7 %shard_map.77 = (bf16[16,64,512]{2,1,0:T(8,128)(2,1)}, bf16[2,3,128,512]{3,2,1,0:T(8,128)(2,1)}) custom-call(s32[448]{0:T(512)} %concatenate.7.tab, bf16[16,64,512]{2,1,0:T(8,128)(2,1)} %bitcast.18, bf16[2,3,128,512]{3,2,1,0:T(8,128)(2,1)} %bitcast.20, bf16[16,64,512]{2,1,0:T(8,128)(2,1)} %bitcast.19), custom_call_target="tpu_custom_call" | custom-call | flops 4000000000 | bytes 6000000 | tf_op jit(solution)/shard_map/pallas_call | solution.py:373
  311.0 2.3 copy.38
  313.3 0.9 copy.39
  (26 shorter events, 0.8 us)
Async XLA Ops:
  0.6 0.7 copy-start.3
  0.6 0.7 copy-start.2
  1.3 0.7 copy-start.1
  22.6 4.4 %collective-permute-start = (s32[16,5]{1,0:T(8,128)S(1)}, s32[16,5]{1,0:T(8,128)S(1)}, u32[]{:S(2)}, u32[]{:S(2)}) collective-permute-start(s32[16,5]{1,0:T(8,128)S(1)} %bitcast.15), channel_id=1, source_target_pairs={{0,128},{8,136},{16,144},{24,152},{32,160},{40,168},{48,176},{56,1... | collective-permute-start | bytes 968 | tf_op jit(solution)/shard_map/ppermute | solution.py:330
  310.9 2.3 copy-start

commit v2 on v1

--- a/solution.py
+++ b/solution.py
@@ -17,18 +17,20 @@
 NONE = -100000
 
 
-def kernel(nz, ch, heads, tab, q_in, kv_in, g_in, att_out, sg_out,
+def kernel(nz, nt, ch, heads, owner_in, entry_in, count_in, q_in, kv_in, g_in, att_out, sg_out,
            kv, q_own, q_nbr, g_own, g_nbr, pb, dpb, rs, fin, asend, arecv, att,
            lse, gp, st_s, st_r, wts, dlt,
            ag_s, ag_r, loc_s, loc_r, qg_s, qg_r, own_l, stx_s, stx_r,
-           rs_s, rs_r, a_s, a_r, f_s, f_r, o_l):
+           rs_s, rs_r, a_s, a_r, f_s, f_r, o_l,
+           meta, made, made_u, tab, tab_u, me_s, me_r, t_l):
     half = nz // 2
     stride = 2 * ch
-    slots = nz * SLOTS
+    per_t = ch // nt
     scaling = HEAD_DIM ** (-0.5)
     q_blk, g_blk = (q_own, q_nbr), (g_own, g_nbr)
     sec = lax.axis_index("section")
     seq = lax.axis_index("seq")
+    ten = lax.axis_index("tensor")
     y, z = lax.div(seq, nz), lax.rem(seq, nz)
     up, down = lax.rem(z + 1, nz), lax.rem(z + nz - 1, nz)
     z_to = (up, down)
@@ -38,6 +40,9 @@
 
     sibling = dev(1 - sec, y, z)
     y_nbr = dev(sec, 1 - y, z)
+
+    def peer(b, dt):
+        return {"seq": (y if b == 0 else 1 - y) * nz + z, "tensor": lax.rem(ten + dt, nt)}
 
     def remote(src, dst, ssem, rsem, device):
         return pltpu.make_async_remote_copy(
@@ -46,13 +51,23 @@
 
     barrier = pltpu.get_barrier_semaphore()
     for device in (sibling, y_nbr, dev(sec, y, up), dev(sec, y, down),
-                   dev(1 - sec, y, up), dev(1 - sec, y, down)):
+                   dev(1 - sec, y, up), dev(1 - sec, y, down)) + tuple(
+                       peer(b, dt) for b in (0, 1) for dt in range(1, nt)):
         pl.semaphore_signal(barrier, inc=1, device_id=device, device_id_type=MESH)
     own_q = pltpu.make_async_copy(q_in, q_own, own_l.at[0])
     own_g = pltpu.make_async_copy(g_in, g_own, own_l.at[1])
     own_q.start()
     own_g.start()
-    pl.semaphore_wait(barrier, 6)
+    lanes8 = lax.broadcasted_iota(jnp.int32, (8, 128), 1)
+    rows8 = lax.broadcasted_iota(jnp.int32, (8, 128), 0)
+    mine = jnp.zeros((8, 128), jnp.int32)
+    for s in range(per_t):
+        for j in range(NEIGH):
+            at = lanes8 == (ten * per_t + s) * NEIGH + j
+            for row, value in enumerate((owner_in[s, j], entry_in[s, j], count_in[s])):
+                mine = jnp.where(jnp.logical_and(at, rows8 == row), value, mine)
+    meta[0, ten] = mine
+    pl.semaphore_wait(barrier, 6 + 2 * (nt - 1))
 
     def place(d, k):
         return nz - k if d == 0 else k
@@ -76,6 +91,10 @@
     locals_ = [remote(kv_in.at[c], kv.at[c, 0], loc_s.at[c], loc_r.at[c], sibling) for c in (0, 1)]
     for copy in locals_:
         copy.start()
+    maps = [remote(meta.at[0, ten], meta.at[b, ten], me_s.at[b, dt], me_r.at[b, dt],
+                   peer(b, dt)) for dt in range(nt) for b in (0, 1) if b + dt > 0]
+    for copy in maps:
+        copy.start()
     swap = [remote(q_in, q_nbr, qg_s.at[0], qg_r.at[0], y_nbr),
             remote(g_in, g_nbr, qg_s.at[1], qg_r.at[1], y_nbr)]
     for copy in swap:
@@ -87,15 +106,63 @@
         rs[d, c, m] = jnp.zeros(rs.shape[3:], rs.dtype)
     lanes = lax.broadcasted_iota(jnp.int32, (SPAN, 128), 1)
 
+    def build_tables():
+        for dt in range(nt):
+            for b in (0, 1):
+                if b + dt > 0:
+                    here = meta.at[b, lax.rem(ten + nt - dt, nt)]
+                    remote(here, here, me_s.at[b, dt], me_r.at[b, dt], peer(b, dt)).wait_recv()
+        unit = lax.broadcasted_iota(jnp.int32, (nz, 128), 1)
+        row = lax.broadcasted_iota(jnp.int32, (nz, 128), 0)
+        made_all = jnp.zeros((nz, 128), jnp.int32)
+        unit_all = jnp.zeros((8, 128), jnp.int32)
+        for b in (0, 1):
+            whole = meta[b, 0]
+            for t in range(1, nt):
+                whole = whole + meta[b, t]
+            spread = lambda i: jnp.broadcast_to(whole[i:i + 1], (nz, 128))
+            owner, entry, count = spread(0), spread(1), spread(2)
+            j_of = lax.bitwise_and(unit, 1)
+            span = lax.shift_right_logical(unit, 1)
+            col = owner - y * nz
+            used = ((unit < ch * NEIGH) & (j_of < count)) & ((col >= 0) & (col < nz))
+            rel = jnp.where(col < z, col - z + nz, col - z)
+            mine = jnp.logical_and(used, rel == row)
+            u0 = jnp.min(jnp.where(mine, unit, 1000), axis=1, keepdims=True)
+            u1 = jnp.max(jnp.where(mine, unit, -1), axis=1, keepdims=True)
+            u1 = jnp.where(u1 == u0, -1, u1)
+            lane = (y if b == 0 else 1 - y) * ch + span
+            for r, u in ((0, u0), (1, u1)):
+                at = unit == u
+                get = lambda v: jnp.sum(jnp.where(at, v, 0), axis=1, keepdims=True)
+                values = (get(span), get(entry)) + tuple(
+                    get(jnp.where(j_of == j, lane - NONE, 0)) + NONE for j in range(NEIGH))
+                for i, value in enumerate(values):
+                    made_all = jnp.where(unit == i * SLOTS + b * 2 + r, value, made_all)
+            rank = jnp.sum(jnp.where(jnp.logical_and(mine, unit != u0), 1, 0), axis=0, keepdims=True)
+            use1, rel1, entry1 = used[0:1], rel[0:1], entry[0:1]
+            for i, value in enumerate((rel1, b * 2 + rank, entry1)):
+                value = jnp.broadcast_to(jnp.where(use1, value, 0), (8, 128))
+                unit_all = jnp.where(rows8 == b * 3 + i, value, unit_all)
+        made[...] = made_all
+        made_u[...] = unit_all
+        copies = [pltpu.make_async_copy(made, tab, t_l.at[0]),
+                  pltpu.make_async_copy(made_u, tab_u, t_l.at[1])]
+        for copy in copies:
+            copy.start()
+        for copy in copies:
+            copy.wait()
+
     def pick(three, es):
         return jnp.where(es == 0, three[0], jnp.where(es == 1, three[1], three[2]))
 
     def fwd_item(n, b):
         idx = jnp.where(lax.rem(n, 2) == 1, nz - lax.div(n + 1, 2), lax.div(n, 2))
         for r in (0, 1):
-            sl = idx * SLOTS + (b * 2 + r)
-            sp, es = tab[sl], tab[slots + sl]
-            l_of = (tab[2 * slots + sl], tab[3 * slots + sl])
+            slot = b * 2 + r
+            sl = idx * SLOTS + slot
+            sp, es = tab[idx, slot], tab[idx, SLOTS + slot]
+            l_of = (tab[idx, 2 * SLOTS + slot], tab[idx, 3 * SLOTS + slot])
             stat_l, stat_g = [], []
             for h in range(heads):
                 hs = pl.ds(h * HEAD_DIM, HEAD_DIM)
@@ -131,6 +198,7 @@
     own_g.wait()
     for copy in locals_:
         copy.wait_recv()
+    build_tables()
     lag = min(4, half)
 
     def nbr_done(k):
@@ -192,9 +260,9 @@
         for slot in range(SLOTS):
             b = slot // 2
             sl = idx * SLOTS + slot
-            sp, es = tab[sl], tab[slots + sl]
-            l0 = tab[2 * slots + sl] + h * stride
-            l1 = tab[3 * slots + sl] + h * stride
+            sp, es = tab[idx, slot], tab[idx, SLOTS + slot]
+            l0 = tab[idx, 2 * SLOTS + slot] + h * stride
+            l1 = tab[idx, 3 * SLOTS + slot] + h * stride
             w = jnp.where(lanes == l0, wts[0], 0.0) + jnp.where(lanes == l1, wts[1], 0.0)
             p = pb[sl, :, hs] * jnp.sum(w, axis=1, keepdims=True)
             if c == 0:
@@ -235,10 +303,10 @@
             hs = pl.ds(h * HEAD_DIM, HEAD_DIM)
             acc = jnp.zeros((SPAN, HEAD_DIM), jnp.float32)
             for j in range(NEIGH):
-                at = 4 * slots + (b * ch + sp) * NEIGH + j
-                sl = tab[at]
-                idx = tab[at + 2 * ch * NEIGH]
-                es = tab[at + 4 * ch * NEIGH]
+                at = sp * NEIGH + j
+                idx = tab_u[b * 3, at]
+                sl = idx * SLOTS + tab_u[b * 3 + 1, at]
+                es = tab_u[b * 3 + 2, at]
                 w = column(wts[j], y_b * ch + sp + h * stride)
                 p = (pb[sl, :, hs] * w).astype(jnp.bfloat16)
                 acc += jnp.dot(p, kv[1, idx, es, :, hs], preferred_element_type=jnp.float32)
@@ -315,47 +383,12 @@
         steps = half + 1 if d == c else half
         lax.fori_loop(2, steps, lambda k, t: (forward(d, c, k).wait_send(), t)[1], 0)
         lax.fori_loop(1, steps, lambda m, t: (step_on(d, c, m).wait_send(), t)[1], 0)
-    for copy in locals_ + swap + [stats, give]:
+    for copy in locals_ + swap + maps + [stats, give]:
         copy.wait_send()
     for copy in finals:
         copy.wait_send()
         copy.wait_recv()
     out_copy.wait()
-
-
-def tables(owner_part, slot_part, count_part, nz):
-    packed = jnp.concatenate([owner_part, slot_part, count_part[:, None]], axis=1)
-    own = lax.all_gather(packed, "tensor", axis=0, tiled=True)
-    size = 2 * nz
-    other = lax.ppermute(own, "seq", [(i, (i + nz) % size) for i in range(size)])
-    meta = jnp.stack([own, other])
-    ch = own.shape[0]
-    seq = lax.axis_index("seq")
-    y, z = seq // nz, seq % nz
-    owner, entry, count = meta[..., 0:2], meta[..., 2:4], meta[..., 4:5]
-    j_of = jnp.broadcast_to(jnp.arange(NEIGH)[None, None, :], owner.shape)
-    used = (j_of < count) & (owner // nz == y)
-    units = ch * NEIGH
-    shape = owner.shape
-    flat = lambda a: jnp.broadcast_to(a, shape).reshape(2, units)
-    owner, entry, used, j_of = flat(owner), flat(entry), flat(used), flat(j_of)
-    span = flat(jnp.arange(ch)[None, :, None])
-    same = (owner[:, :, None] == owner[:, None, :]) & used[:, None, :]
-    earlier = jnp.arange(units)[None, :] < jnp.arange(units)[:, None]
-    rank = jnp.sum((same & earlier).astype(jnp.int32), axis=2)
-    rel = (owner - z) % nz
-    block = jnp.arange(2)[:, None]
-    dest = rel * SLOTS + block * 2 + rank
-    y_b = jnp.where(block == 0, y, 1 - y)
-    lane = y_b * ch + span
-    slots = nz * SLOTS
-    match = ((dest[None] == jnp.arange(slots)[:, None, None]) & used[None]).astype(jnp.int32)
-    total = lambda a: jnp.sum(match * a, axis=(1, 2))
-    lane_of = [total((lane - NONE) * (j_of == j)) + NONE for j in range(NEIGH)]
-    dest = jnp.where(used, dest, 0)
-    parts = [total(span), total(entry), lane_of[0], lane_of[1],
-             dest.reshape(-1), (dest // SLOTS).reshape(-1), jnp.where(used, entry, 0).reshape(-1)]
-    return jnp.concatenate(parts).astype(jnp.int32)
 
 
 def per_device(nz, queries, store_kv, out_grad, neighbour_owner, neighbour_slot, neighbour_count):
@@ -364,16 +397,16 @@
     ch = rows // SPAN
     half = nz // 2
     entries = store_kv.shape[1] // NLEN
-    tab = tables(neighbour_owner, neighbour_slot, neighbour_count, nz)
+    nt = lax.axis_size("tensor")
     bf, f32 = jnp.bfloat16, jnp.float32
     dma = pltpu.SemaphoreType.DMA
     block = (entries, NLEN, width)
     spans = (ch, SPAN, width)
     any_spec = pl.BlockSpec(memory_space=pl.ANY)
     attended, store_grad = pl.pallas_call(
-        functools.partial(kernel, nz, ch, heads),
+        functools.partial(kernel, nz, nt, ch, heads),
         out_shape=[jax.ShapeDtypeStruct(spans, bf), jax.ShapeDtypeStruct((2,) + block, bf)],
-        in_specs=[pl.BlockSpec(memory_space=pltpu.SMEM), any_spec, any_spec, any_spec],
+        in_specs=[pl.BlockSpec(memory_space=pltpu.SMEM)] * 3 + [any_spec, any_spec, any_spec],
         out_specs=[any_spec, any_spec],
         scratch_shapes=[
             pltpu.VMEM((2, nz) + block, bf),
@@ -391,12 +424,15 @@
             dma((2,)), dma((2,)), dma((2,)), dma((1,)), dma((1,)),
             dma((2, 2, half + 1)), dma((2, 2, half + 1)), dma((1,)), dma((1,)),
             dma((2,)), dma((2,)), dma((1,)),
+            pltpu.VMEM((2, nt, 8, 128), jnp.int32), pltpu.VMEM((nz, 128), jnp.int32),
+            pltpu.VMEM((8, 128), jnp.int32), pltpu.SMEM((nz, 128), jnp.int32),
+            pltpu.SMEM((8, 128), jnp.int32), dma((2, nt)), dma((2, nt)), dma((2,)),
         ],
         compiler_params=pltpu.CompilerParams(
             collective_id=0, has_side_effects=True, vmem_limit_bytes=60 * 1024 * 1024),
         cost_estimate=pl.CostEstimate(flops=4 * 10 ** 9, bytes_accessed=6 * 10 ** 6,
                                       transcendentals=4 * 10 ** 6),
-    )(tab, queries.reshape(spans), store_kv.reshape((2,) + block), out_grad.reshape(spans))
+    )(neighbour_owner, neighbour_slot, neighbour_count, queries.reshape(spans), store_kv.reshape((2,) + block), out_grad.reshape(spans))
     return attended.reshape(rows, width), store_grad.reshape(store_kv.shape)
 
 

time: 314 us -> 284 us (0.904)
  blocking collectives: 20.5 us -> 0 us
  local copies, waits for them, and re-layouts: 6.85 us -> 3.22 us
    all_gather x1 -> x0, blocking collectives: 20.5 us -> none  [tables(): own = lax.all_gather(packed, 'tensor', axis=0, tiled=True)]
  transfers between devices with their start and end apart: 1 -> 0, of which waited for: 1 -> 0; matrix products, arithmetic and copies ran while one was open for 0% -> 0% of each run, Pallas kernels for 0% -> 0%
where the time goes in v2:
time: 284 us
  Pallas kernels  280 us (99%)
  local copies, waits for them, and re-layouts  3.22 us (1%)
    pallas_call x1, Pallas kernels, per_device(): pl.pallas_call(functools.partial(kernel, nz, nt, ch, heads), out_shape=[j...  280 us

profile of v2, /device:TPU:1, one launch (start us, length us, event | category | flops | bytes accessed | tf_op | source)
XLA Modules:
  0.0 284.0 jit_solution(11113362116444087480)
XLA Ops:
  0.6 280.1 %shard_map.77 = (bf16[16,64,512]{2,1,0:T(8,128)(2,1)}, bf16[2,3,128,512]{3,2,1,0:T(8,128)(2,1)}) custom-call(s32[2,2]{1,0:T(2,128)} %owner_in.1, s32[2,2]{1,0:T(2,128)} %entry_in.1, s32[2]{0:T(128)} %count_in.1, bf16[16,64,512]{2,1,0:T(8,128)(2,1)} %bitcast.7, bf16[2,3,128,512]{3,2,1,0:T(8,128)(2,1)} %bitcast.9, bf16[16,64,512]{2,1,0:T(8,128)(2,1)} %bitcast.8), custom_call_target="tpu_custom_call" | custom-call | flops 4000000000 | bytes 6000000 | tf_op jit(solution)/shard_map/pallas_call | solution.py:406
  280.8 0.0 copy-start
  280.8 2.3 copy.10
  283.1 0.0 copy-done
  283.1 0.9 copy.11
Async XLA Ops:
  280.8 2.3 copy-start

commit v3 on v2

--- a/solution.py
+++ b/solution.py
@@ -18,7 +18,7 @@
 
 
 def kernel(nz, nt, ch, heads, owner_in, entry_in, count_in, q_in, kv_in, g_in, att_out, sg_out,
-           kv, q_own, q_nbr, g_own, g_nbr, pb, dpb, rs, fin, asend, arecv, att,
+           kv, q_own, q_nbr, g_own, g_nbr, pb, dpb, rs, cbuf, fin, asend, arecv, att,
            lse, gp, st_s, st_r, wts, dlt,
            ag_s, ag_r, loc_s, loc_r, qg_s, qg_r, own_l, stx_s, stx_r,
            rs_s, rs_r, a_s, a_r, f_s, f_r, o_l,
@@ -72,22 +72,39 @@
     def place(d, k):
         return nz - k if d == 0 else k
 
-    def first(d, c):
-        return remote(kv_in.at[c], kv.at[c, place(d, 1)], ag_s.at[d, c, 1], ag_r.at[d, c, 1],
-                      dev(1 - sec, y, z_to[d]))
-
-    def forward(d, c, k):
-        return remote(kv.at[c, place(d, k - 1)], kv.at[c, place(d, k)], ag_s.at[d, c, k],
-                      ag_r.at[d, c, k], dev(sec, y, z_to[d]))
-
-    def arrived(d, c, k):
-        here = kv.at[c, place(d, k)]
-        remote(here, here, ag_s.at[d, c, k], ag_r.at[d, c, k], dev(sec, y, z_to[d])).wait_recv()
-
-    first(0, 0).start()
-    first(1, 1).start()
-    first(0, 1).start()
-    first(1, 0).start()
+    def far(c, e):
+        return 0 if e < 2 - c else 1
+
+    def first(d, c, e):
+        return remote(kv_in.at[c, e], kv.at[c, place(d, 1), e], ag_s.at[d, c, 1, e],
+                      ag_r.at[d, c, 1, e], dev(1 - sec, y, z_to[d]))
+
+    def forward(d, c, k, e):
+        return remote(kv.at[c, place(d, k - 1), e], kv.at[c, place(d, k), e], ag_s.at[d, c, k, e],
+                      ag_r.at[d, c, k, e], dev(sec, y, z_to[d]))
+
+    def arrived(d, c, k, e):
+        here = kv.at[c, place(d, k), e]
+        remote(here, here, ag_s.at[d, c, k, e], ag_r.at[d, c, k, e],
+               dev(sec, y, z_to[d])).wait_recv()
+
+    def pass_on(c, k, e):
+        for d in (0, 1):
+            arrived(d, c, k, e)
+            if not isinstance(k, int) or k != half - 1 or far(c, e) == d:
+                forward(d, c, k + 1, e).start()
+
+    def start_gather():
+        for e in range(3):
+            for c in (0, 1):
+                for d in (0, 1):
+                    first(d, c, e).start()
+
+    def end_gather(c):
+        for e in range(3):
+            arrived(far(c, e), c, half, e)
+
+    start_gather()
     locals_ = [remote(kv_in.at[c], kv.at[c, 0], loc_s.at[c], loc_r.at[c], sibling) for c in (0, 1)]
     for copy in locals_:
         copy.start()
@@ -102,8 +119,6 @@
 
     lse[...] = jnp.full_like(lse, DEAD)
     gp[...] = jnp.zeros_like(gp)
-    for d, c, m in ((0, 0, half), (1, 1, half), (0, 1, half - 1), (1, 0, half - 1)):
-        rs[d, c, m] = jnp.zeros(rs.shape[3:], rs.dtype)
     lanes = lax.broadcasted_iota(jnp.int32, (SPAN, 128), 1)
 
     def build_tables():
@@ -156,100 +171,134 @@
     def pick(three, es):
         return jnp.where(es == 0, three[0], jnp.where(es == 1, three[1], three[2]))
 
-    def fwd_item(n, b):
-        idx = jnp.where(lax.rem(n, 2) == 1, nz - lax.div(n + 1, 2), lax.div(n, 2))
+    def place_of(n):
+        return jnp.where(lax.rem(n, 2) == 1, nz - lax.div(n + 1, 2), lax.div(n, 2))
+
+    def insert(ref, idx, slot, columns):
+        for j in range(NEIGH):
+            lane = tab[idx, (2 + j) * SLOTS + slot]
+            a = ref[j]
+            for h in range(heads):
+                a = jnp.where(lanes == lane + h * stride, columns[h], a)
+            ref[j] = a
+
+    def score_item(n, b):
+        idx = place_of(n)
         for r in (0, 1):
             slot = b * 2 + r
             sl = idx * SLOTS + slot
             sp, es = tab[idx, slot], tab[idx, SLOTS + slot]
-            l_of = (tab[idx, 2 * SLOTS + slot], tab[idx, 3 * SLOTS + slot])
-            stat_l, stat_g = [], []
+            columns = []
             for h in range(heads):
                 hs = pl.ds(h * HEAD_DIM, HEAD_DIM)
-                qv = q_blk[b][sp, :, hs]
-                gv = g_blk[b][sp, :, hs]
                 ks = pick([kv[0, idx, e, :, hs] for e in range(3)], es)
-                vs = pick([kv[1, idx, e, :, hs] for e in range(3)], es)
-                s = lax.dot_general(qv, ks, (((1,), (1,)), ((), ())),
+                s = lax.dot_general(q_blk[b][sp, :, hs], ks, (((1,), (1,)), ((), ())),
                                     preferred_element_type=jnp.float32) * scaling
-                dp = lax.dot_general(gv, vs, (((1,), (1,)), ((), ())),
-                                     preferred_element_type=jnp.float32)
                 top = jnp.max(s, axis=1, keepdims=True)
                 p = jnp.exp(s - top)
                 tot = jnp.sum(p, axis=1, keepdims=True)
-                p = p * (1.0 / tot)
-                pb[sl, :, hs] = p
+                pb[sl, :, hs] = p * (1.0 / tot)
+                columns.append(top + jnp.log(tot))
+            insert(lse, idx, slot, columns)
+
+    def grad_item(n, b):
+        idx = place_of(n)
+        for r in (0, 1):
+            slot = b * 2 + r
+            sl = idx * SLOTS + slot
+            sp, es = tab[idx, slot], tab[idx, SLOTS + slot]
+            columns = []
+            for h in range(heads):
+                hs = pl.ds(h * HEAD_DIM, HEAD_DIM)
+                vs = pick([kv[1, idx, e, :, hs] for e in range(3)], es)
+                dp = lax.dot_general(g_blk[b][sp, :, hs], vs, (((1,), (1,)), ((), ())),
+                                     preferred_element_type=jnp.float32)
                 dpb[sl, :, hs] = dp
-                stat_l.append(top + jnp.log(tot))
-                stat_g.append(jnp.sum(p * dp, axis=1, keepdims=True))
-            for j in range(NEIGH):
-                a, g2 = lse[j], gp[j]
-                for h in range(heads):
-                    hit = lanes == l_of[j] + h * stride
-                    a = jnp.where(hit, stat_l[h], a)
-                    g2 = jnp.where(hit, stat_g[h], g2)
-                lse[j] = a
-                gp[j] = g2
-
-    def items(lo, hi, b):
-        lax.fori_loop(lo, hi, lambda n, t: (fwd_item(n, b), t)[1], 0)
+                columns.append(jnp.sum(pb[sl, :, hs] * dp, axis=1, keepdims=True))
+            insert(gp, idx, slot, columns)
+
+    def items(work, lo, hi, b):
+        lax.fori_loop(lo, hi, lambda n, t: (work(n, b), t)[1], 0)
 
     own_q.wait()
     own_g.wait()
     for copy in locals_:
         copy.wait_recv()
     build_tables()
-    lag = min(4, half)
-
-    def nbr_done(k):
-        return jnp.minimum(jnp.maximum((k + 1 - lag) * 4, 0), 2 * half - 3)
+    lag = 4
+
+    def done(k):
+        return jnp.maximum((k + 1 - lag) * 4, 0)
+
+    def upto(step):
+        return max(2 * step + 1, 0)
 
     def gather_step(k, t):
-        for d, c in ((0, 0), (1, 1)):
-            arrived(d, c, k)
-            forward(d, c, k + 1).start()
-        items(jnp.maximum(2 * k - 3, 0), 2 * k - 1, 0)
-        for d, c in ((0, 1), (1, 0)):
-            arrived(d, c, k)
-
-            @pl.when(k + 1 < half)
-            def _():
-                forward(d, c, k + 1).start()
+        pass_on(0, k, 0)
+        items(score_item, jnp.maximum(2 * k - 3, 0), 2 * k - 1, 0)
+        pass_on(1, k, 0)
 
         @pl.when(k == lag)
         def _():
             for copy in swap:
                 copy.wait_recv()
 
-        items(nbr_done(k - 1), nbr_done(k), 1)
+        lo, hi = done(k - 1), done(k)
+        mid = jnp.minimum(lo + 2, hi)
+        items(score_item, lo, mid, 1)
+        pass_on(0, k, 1)
+        items(score_item, mid, hi, 1)
+        pass_on(1, k, 1)
+        items(grad_item, lo, hi, 0)
+        pass_on(0, k, 2)
+        items(grad_item, lo, hi, 1)
+        pass_on(1, k, 2)
         return t
 
-    lax.fori_loop(1, half, gather_step, 0)
-    if half <= lag:
+    both = half - 3
+    lax.fori_loop(1, both + 1, gather_step, 0)
+    if both < lag:
         for copy in swap:
             copy.wait_recv()
-    items(2 * half - 3, 2 * half - 1, 0)
-    items(nbr_done(half - 1), 2 * half - 1, 1)
-    arrived(0, 0, half)
-    arrived(1, 1, half)
-    fwd_item(2 * half - 1, 0)
-    fwd_item(2 * half - 1, 1)
+    own_at = upto(both - 1)
+    nbr_at = max((both + 1 - lag) * 4, 0)
+    if half > 2:
+        for e in range(3):
+            pass_on(0, half - 2, e)
+        pass_on(1, half - 2, 0)
+    items(score_item, own_at, upto(both), 0)
+    items(score_item, nbr_at, upto(both), 1)
+    for e in range(3):
+        pass_on(0, half - 1, e)
+    if half > 2:
+        pass_on(1, half - 2, 1)
+        pass_on(1, half - 2, 2)
+    for b in (0, 1):
+        items(score_item, upto(both), upto(half - 1), b)
+    for b in (0, 1):
+        items(grad_item, nbr_at, upto(half - 2), b)
+    end_gather(0)
+    for b in (0, 1):
+        items(score_item, upto(half - 1), 2 * half, b)
+
+    def exchange(i, value):
+        st_s[i] = value
+        copy = remote(st_s.at[i], st_r.at[i], stx_s.at[i], stx_r.at[i], y_nbr)
+        copy.start()
+        copy.wait_recv()
+        return copy
 
     a0, a1 = lse[0], lse[1]
     top = jnp.maximum(a0, a1)
     lc = top + jnp.log(jnp.exp(a0 - top) + jnp.exp(a1 - top))
-    gc = jnp.exp(a0 - lc) * gp[0] + jnp.exp(a1 - lc) * gp[1]
-    st_s[0] = lc
-    st_s[1] = gc
-    stats = remote(st_s, st_r, stx_s.at[0], stx_r.at[0], y_nbr)
-    stats.start()
-    stats.wait_recv()
-    lo_, go_ = st_r[0], st_r[1]
+    stats = [exchange(0, lc)]
+    lo_ = st_r[0]
     top = jnp.maximum(lc, lo_)
     total = top + jnp.log(jnp.exp(lc - top) + jnp.exp(lo_ - top))
-    dlt[...] = jnp.exp(lc - total) * gc + jnp.exp(lo_ - total) * go_
     wts[0] = jnp.exp(a0 - total)
     wts[1] = jnp.exp(a1 - total)
+    for e in range(3):
+        pass_on(1, half - 1, e)
 
     def column(values, lane):
         return jnp.sum(jnp.where(lanes == lane, values, 0.0), axis=1, keepdims=True)
@@ -279,22 +328,48 @@
             out = out * scaling
         return out.reshape(3, NLEN, HEAD_DIM)
 
-    def step_on(d, c, m):
-        zz = lax.rem(z + 1 + d * (nz - 2), nz)
-        return remote(rs.at[d, c, m], rs.at[d, c, m - 1], rs_s.at[d, c, m - 1],
-                      rs_r.at[d, c, m - 1], dev(sec, y, zz))
-
-    def sum_arrived(d, c, m):
-        here = rs.at[d, c, m]
-        remote(here, here, rs_s.at[d, c, m], rs_r.at[d, c, m], y_nbr).wait_recv()
-
-    def chunk(d, c, m):
-        idx = jnp.where(d == 0, m, nz - m)
+    def contribute(c, idx, into):
         for h in range(heads):
-            hs = pl.ds(h * HEAD_DIM, HEAD_DIM)
-            o = contribution(c, idx, h) + rs[d, c, m, :, :, hs].astype(jnp.float32)
-            rs[d, c, m, :, :, hs] = o.astype(jnp.bfloat16)
-        step_on(d, c, m).start()
+            cbuf[c, into, :, :, pl.ds(h * HEAD_DIM, HEAD_DIM)] = contribution(c, idx, h)
+
+    def step_on(d, c, m, e):
+        return remote(rs.at[d, c, m, e], rs.at[d, c, m - 1, e], rs_s.at[d, c, m - 1, e],
+                      rs_r.at[d, c, m - 1, e], dev(sec, y, z_to[d]))
+
+    def sum_arrived(d, c, m, e):
+        here = rs.at[d, c, m, e]
+        remote(here, here, rs_s.at[d, c, m, e], rs_r.at[d, c, m, e], y_nbr).wait_recv()
+
+    def contribute_both(c, m):
+        lax.fori_loop(0, 2, lambda d, t: (contribute(c, jnp.where(d == 0, m, nz - m), d), t)[1], 0)
+
+    def start_sums(c):
+        contribute(c, half, 0)
+        for e in range(3):
+            d = far(c, e)
+            rs[d, c, half, e] = cbuf[c, 0, e].astype(jnp.bfloat16)
+            step_on(d, c, half, e).start()
+        contribute_both(c, half - 1)
+        for e in range(3):
+            d = 1 - far(c, e)
+            rs[d, c, half - 1, e] = cbuf[c, d, e].astype(jnp.bfloat16)
+            step_on(d, c, half - 1, e).start()
+
+    def add_on(c, d, m, e):
+        sum_arrived(d, c, m, e)
+        o = cbuf[c, d, e] + rs[d, c, m, e].astype(jnp.float32)
+        rs[d, c, m, e] = o.astype(jnp.bfloat16)
+        step_on(d, c, m, e).start()
+
+    def last_sum(c, e):
+        sum_arrived(0, c, 0, e)
+        sum_arrived(1, c, 0, e)
+        o = cbuf[c, 0, e] + (rs[0, c, 0, e].astype(jnp.float32) + rs[1, c, 0, e].astype(jnp.float32))
+        fin[c, e] = o.astype(jnp.bfloat16)
+        give_back(c, e).start()
+
+    def give_back(c, e):
+        return remote(fin.at[c, e], sg_out.at[c, e], f_s.at[c, e], f_r.at[c, e], sibling)
 
     def attended_span(b, sp):
         y_b = y if b == 0 else 1 - y
@@ -325,69 +400,81 @@
         return t
 
     give = remote(asend, arecv, a_s.at[0], a_r.at[0], y_nbr)
-    events = 2 * half - 1
-    per = -(-ch // 4)
-
-    def sum_step(e, t):
-        odd = lax.rem(e, 2)
-        m = half - lax.div(e + 1, 2)
-        for c in (0, 1):
-            d = odd if c == 0 else 1 - odd
-
-            @pl.when(e >= 2)
-            def _():
-                sum_arrived(d, c, m)
-
-            chunk(d, c, m)
-        if events >= 15:
-            @pl.when(jnp.logical_and(e >= 1, e <= 4))
-            def _():
-                lax.fori_loop((e - 1) * per, e * per, nbr_span, 0)
-
-            @pl.when(e == 4)
-            def _():
-                give.start()
-
-            @pl.when(e == 9)
-            def _():
-                give.wait_recv()
-
-            @pl.when(jnp.logical_and(e >= 9, e <= 12))
-            def _():
-                lax.fori_loop((e - 9) * per, (e - 8) * per, own_span, 0)
+    out_copy = pltpu.make_async_copy(att, att_out, o_l.at[0])
+
+    start_sums(1)
+    end_gather(1)
+    for b in (0, 1):
+        items(grad_item, upto(half - 2), 2 * half, b)
+    gc = wts[0] * gp[0] + wts[1] * gp[1]
+    stats.append(exchange(1, gc))
+    dlt[...] = gc + st_r[1]
+    start_sums(0)
+    for e in range(3):
+        for c in (1, 0):
+            add_on(c, far(c, e), half - 1, e)
+
+    def spans(k):
+        if half < 8:
+            return
+
+        @pl.when(k <= 3)
+        def _():
+            lax.fori_loop((k - 2) * (ch // 2), (k - 1) * (ch // 2), nbr_span, 0)
+
+        @pl.when(k == 3)
+        def _():
+            give.start()
+
+        @pl.when(k == 6)
+        def _():
+            give.wait_recv()
+
+        @pl.when(jnp.logical_and(k >= 6, k <= 7))
+        def _():
+            lax.fori_loop((k - 6) * (ch // 2), (k - 5) * (ch // 2), own_span, 0)
+
+        @pl.when(k == 7)
+        def _():
+            out_copy.start()
+
+    def sum_step(k, t):
+        m = half - k
+        contribute_both(1, m)
+        contribute_both(0, m)
+        for e in range(3):
+            for c in (1, 0):
+                for d in (0, 1):
+                    add_on(c, d, m, e)
+        spans(k)
         return t
 
-    lax.fori_loop(0, events, sum_step, 0)
-    if events < 15:
+    lax.fori_loop(2, half, sum_step, 0)
+    if half < 8:
         lax.fori_loop(0, ch, nbr_span, 0)
         give.start()
         give.wait_recv()
         lax.fori_loop(0, ch, own_span, 0)
-    out_copy = pltpu.make_async_copy(att, att_out, o_l.at[0])
-    out_copy.start()
-    finals = []
-    for c in (1, 0):
-        sum_arrived(0, c, 0)
-        sum_arrived(1, c, 0)
-        for h in range(heads):
-            hs = pl.ds(h * HEAD_DIM, HEAD_DIM)
-            o = contribution(c, 0, h) + (rs[0, c, 0, :, :, hs].astype(jnp.float32)
-                                         + rs[1, c, 0, :, :, hs].astype(jnp.float32))
-            fin[c, :, :, hs] = o.astype(jnp.bfloat16)
-        copy = remote(fin.at[c], sg_out.at[c], f_s.at[c], f_r.at[c], sibling)
-        copy.start()
-        finals.append(copy)
-
-    for d, c in ((0, 0), (1, 1), (0, 1), (1, 0)):
-        first(d, c).wait_send()
-        steps = half + 1 if d == c else half
-        lax.fori_loop(2, steps, lambda k, t: (forward(d, c, k).wait_send(), t)[1], 0)
-        lax.fori_loop(1, steps, lambda m, t: (step_on(d, c, m).wait_send(), t)[1], 0)
-    for copy in locals_ + swap + maps + [stats, give]:
+        out_copy.start()
+    contribute(1, 0, 0)
+    contribute(0, 0, 0)
+    for e in range(3):
+        for c in (1, 0):
+            last_sum(c, e)
+
+    for c in (0, 1):
+        for d in (0, 1):
+            for e in range(3):
+                first(d, c, e).wait_send()
+                steps = half + 1 if far(c, e) == d else half
+                lax.fori_loop(2, steps, lambda k, t: (forward(d, c, k, e).wait_send(), t)[1], 0)
+                lax.fori_loop(1, steps, lambda m, t: (step_on(d, c, m, e).wait_send(), t)[1], 0)
+    for copy in locals_ + swap + maps + stats + [give]:
         copy.wait_send()
-    for copy in finals:
-        copy.wait_send()
-        copy.wait_recv()
+    for c in (0, 1):
+        for e in range(3):
+            give_back(c, e).wait_send()
+            give_back(c, e).wait_recv()
     out_copy.wait()
 
 
@@ -415,15 +502,16 @@
             pltpu.VMEM((nz * SLOTS, SPAN, width), f32),
             pltpu.VMEM((nz * SLOTS, SPAN, width), f32),
             pltpu.VMEM((2, 2, half + 1) + block, bf),
+            pltpu.VMEM((2, 2) + block, f32),
             pltpu.VMEM((2,) + block, bf),
             pltpu.VMEM(spans, bf), pltpu.VMEM(spans, bf), pltpu.VMEM(spans, bf),
             pltpu.VMEM((2, SPAN, 128), f32), pltpu.VMEM((2, SPAN, 128), f32),
             pltpu.VMEM((2, SPAN, 128), f32), pltpu.VMEM((2, SPAN, 128), f32),
             pltpu.VMEM((2, SPAN, 128), f32), pltpu.VMEM((SPAN, 128), f32),
-            dma((2, 2, half + 1)), dma((2, 2, half + 1)), dma((2,)), dma((2,)),
-            dma((2,)), dma((2,)), dma((2,)), dma((1,)), dma((1,)),
-            dma((2, 2, half + 1)), dma((2, 2, half + 1)), dma((1,)), dma((1,)),
-            dma((2,)), dma((2,)), dma((1,)),
+            dma((2, 2, half + 1, 3)), dma((2, 2, half + 1, 3)), dma((2,)), dma((2,)),
+            dma((2,)), dma((2,)), dma((2,)), dma((2,)), dma((2,)),
+            dma((2, 2, half + 1, 3)), dma((2, 2, half + 1, 3)), dma((1,)), dma((1,)),
+            dma((2, 3)), dma((2, 3)), dma((1,)),
             pltpu.VMEM((2, nt, 8, 128), jnp.int32), pltpu.VMEM((nz, 128), jnp.int32),
             pltpu.VMEM((8, 128), jnp.int32), pltpu.SMEM((nz, 128), jnp.int32),
             pltpu.SMEM((8, 128), jnp.int32), dma((2, nt)), dma((2, nt)), dma((2,)),

time: 284 us -> 281 us (0.989)
  Pallas kernels: 280 us -> 277 us
    pallas_call x1, Pallas kernels: 280 us -> 277 us  [per_device(): pl.pallas_call(functools.partial(kernel, nz, nt, ch, heads), out_shape=[j...]
where the time goes in v3:
time: 281 us
  Pallas kernels  277 us (99%)
  local copies, waits for them, and re-layouts  3.22 us (1%)
    pallas_call x1, Pallas kernels, per_device(): pl.pallas_call(functools.partial(kernel, nz, nt, ch, heads), out_shape=[j...  277 us

profile of v3, /device:TPU:1, one launch (start us, length us, event | category | flops | bytes accessed | tf_op | source)
XLA Modules:
  0.0 280.9 jit_solution(12904206250387146259)
XLA Ops:
  0.6 277.0 %shard_map.77 = (bf16[16,64,512]{2,1,0:T(8,128)(2,1)}, bf16[2,3,128,512]{3,2,1,0:T(8,128)(2,1)}) custom-call(s32[2,2]{1,0:T(2,128)} %owner_in.1, s32[2,2]{1,0:T(2,128)} %entry_in.1, s32[2]{0:T(128)} %count_in.1, bf16[16,64,512]{2,1,0:T(8,128)(2,1)} %bitcast.7, bf16[2,3,128,512]{3,2,1,0:T(8,128)(2,1)} %bitcast.9, bf16[16,64,512]{2,1,0:T(8,128)(2,1)} %bitcast.8), custom_call_target="tpu_custom_call" | custom-call | flops 4000000000 | bytes 6000000 | tf_op jit(solution)/shard_map/pallas_call | solution.py:493
  277.6 0.0 copy-start
  277.7 2.3 copy.10
  280.0 0.0 copy-done
  280.0 0.9 copy.11
Async XLA Ops:
  277.6 2.3 copy-start

commit v4 on v3

--- a/solution.py
+++ b/solution.py
@@ -22,7 +22,8 @@
            lse, gp, st_s, st_r, wts, dlt,
            ag_s, ag_r, loc_s, loc_r, qg_s, qg_r, own_l, stx_s, stx_r,
            rs_s, rs_r, a_s, a_r, f_s, f_r, o_l,
-           meta, made, made_u, tab, tab_u, me_s, me_r, t_l):
+           meta, made, made_u, tab, tab_u, me_s, me_r, t_l,
+           far_q, far_g, far_made, far_tab, far_st, far_a, fx_s, fx_r, ft_l):
     half = nz // 2
     stride = 2 * ch
     per_t = ch // nt
@@ -72,9 +73,6 @@
     def place(d, k):
         return nz - k if d == 0 else k
 
-    def far(c, e):
-        return 0 if e < 2 - c else 1
-
     def first(d, c, e):
         return remote(kv_in.at[c, e], kv.at[c, place(d, 1), e], ag_s.at[d, c, 1, e],
                       ag_r.at[d, c, 1, e], dev(1 - sec, y, z_to[d]))
@@ -91,7 +89,7 @@
     def pass_on(c, k, e):
         for d in (0, 1):
             arrived(d, c, k, e)
-            if not isinstance(k, int) or k != half - 1 or far(c, e) == d:
+            if not isinstance(k, int) or k < half - 1:
                 forward(d, c, k + 1, e).start()
 
     def start_gather():
@@ -99,10 +97,6 @@
             for c in (0, 1):
                 for d in (0, 1):
                     first(d, c, e).start()
-
-    def end_gather(c):
-        for e in range(3):
-            arrived(far(c, e), c, half, e)
 
     start_gather()
     locals_ = [remote(kv_in.at[c], kv.at[c, 0], loc_s.at[c], loc_r.at[c], sibling) for c in (0, 1)]
@@ -171,6 +165,67 @@
     def pick(three, es):
         return jnp.where(es == 0, three[0], jnp.where(es == 1, three[1], three[2]))
 
+    def far_at(f):
+        return half - 1 + 2 * f
+
+    def far_copy(i, b, src, dst, back):
+        return remote(src, dst, fx_s.at[i, b], fx_r.at[i, b],
+                      dev(sec, y, z_to[1 - b] if back else z_to[b]))
+
+    def far_spans(i, b):
+        ref = (far_q, far_g)[i]
+        return far_copy(i, b, ref.at[0, b], ref.at[1, b], False)
+
+    def far_table(b):
+        return far_copy(2, b, made, far_made.at[b], False)
+
+    def far_tile(i, b):
+        return far_copy(3 + i, b, far_st.at[0, i, b], far_st.at[1, i, b], i < 2)
+
+    def far_part(b):
+        return far_copy(7, b, far_a.at[0, b], far_a.at[1, b], True)
+
+    def send_far():
+        for b in (0, 1):
+            for r in (0, 1):
+                sp = tab[half, b * 2 + r]
+                far_q[0, b, r] = q_blk[b][sp]
+                far_g[0, b, r] = g_blk[b][sp]
+        for b in (0, 1):
+            far_table(b).start()
+            far_spans(0, b).start()
+            far_spans(1, b).start()
+
+    def take_far():
+        for b in (0, 1):
+            far_table(b).wait_recv()
+            pltpu.make_async_copy(far_made.at[b], far_tab.at[b], ft_l.at[b]).start()
+        for b in (0, 1):
+            pltpu.make_async_copy(far_made.at[b], far_tab.at[b], ft_l.at[b]).wait()
+            far_spans(0, b).wait_recv()
+            far_spans(1, b).wait_recv()
+
+    def far_send(i, work):
+        for f in (0, 1):
+            tile = jnp.zeros((SPAN, 128), jnp.float32)
+            for r in (0, 1):
+                for h, value in enumerate(work(f, r)):
+                    tile = jnp.where(lanes == r * heads + h, value, tile)
+            far_st[0, i, f] = tile
+            far_tile(i, f).start()
+
+    def column(values, lane):
+        return jnp.sum(jnp.where(lanes == lane, values, 0.0), axis=1, keepdims=True)
+
+    def far_get(i, f, r, h):
+        return column(far_st[1, i, f], r * heads + h)
+
+    def far_insert(i, ref):
+        for b in (0, 1):
+            far_tile(i, b).wait_recv()
+            for r in (0, 1):
+                insert(ref, half, b * 2 + r, [far_get(i, b, r, h) for h in range(heads)])
+
     def place_of(n):
         return jnp.where(lax.rem(n, 2) == 1, nz - lax.div(n + 1, 2), lax.div(n, 2))
 
@@ -182,40 +237,51 @@
                 a = jnp.where(lanes == lane + h * stride, columns[h], a)
             ref[j] = a
 
-    def score_item(n, b):
+    def score_slot(idx, sl, es, q_of):
+        columns = []
+        for h in range(heads):
+            hs = pl.ds(h * HEAD_DIM, HEAD_DIM)
+            ks = pick([kv[0, idx, e, :, hs] for e in range(3)], es)
+            s = lax.dot_general(q_of(hs), ks, (((1,), (1,)), ((), ())),
+                                preferred_element_type=jnp.float32) * scaling
+            top = jnp.max(s, axis=1, keepdims=True)
+            p = jnp.exp(s - top)
+            tot = jnp.sum(p, axis=1, keepdims=True)
+            pb[sl, :, hs] = p * (1.0 / tot)
+            columns.append(top + jnp.log(tot))
+        return columns
+
+    def grad_slot(idx, sl, es, g_of):
+        columns = []
+        for h in range(heads):
+            hs = pl.ds(h * HEAD_DIM, HEAD_DIM)
+            vs = pick([kv[1, idx, e, :, hs] for e in range(3)], es)
+            dp = lax.dot_general(g_of(hs), vs, (((1,), (1,)), ((), ())),
+                                 preferred_element_type=jnp.float32)
+            dpb[sl, :, hs] = dp
+            columns.append(jnp.sum(pb[sl, :, hs] * dp, axis=1, keepdims=True))
+        return columns
+
+    def item(n, b, slot_work, rows, ref):
         idx = place_of(n)
         for r in (0, 1):
             slot = b * 2 + r
-            sl = idx * SLOTS + slot
-            sp, es = tab[idx, slot], tab[idx, SLOTS + slot]
-            columns = []
-            for h in range(heads):
-                hs = pl.ds(h * HEAD_DIM, HEAD_DIM)
-                ks = pick([kv[0, idx, e, :, hs] for e in range(3)], es)
-                s = lax.dot_general(q_blk[b][sp, :, hs], ks, (((1,), (1,)), ((), ())),
-                                    preferred_element_type=jnp.float32) * scaling
-                top = jnp.max(s, axis=1, keepdims=True)
-                p = jnp.exp(s - top)
-                tot = jnp.sum(p, axis=1, keepdims=True)
-                pb[sl, :, hs] = p * (1.0 / tot)
-                columns.append(top + jnp.log(tot))
-            insert(lse, idx, slot, columns)
+            sp = tab[idx, slot]
+            insert(ref, idx, slot, slot_work(idx, idx * SLOTS + slot, tab[idx, SLOTS + slot],
+                                             lambda hs: rows[b][sp, :, hs]))
+
+    def far_entry(f, r):
+        return far_tab[f, half, SLOTS + f * 2 + r]
+
+    def far_slot(slot_work, rows):
+        return lambda f, r: slot_work(far_at(f), half * SLOTS + f * 2 + r, far_entry(f, r),
+                                      lambda hs: rows[1, f, r, :, hs])
+
+    def score_item(n, b):
+        item(n, b, score_slot, q_blk, lse)
 
     def grad_item(n, b):
-        idx = place_of(n)
-        for r in (0, 1):
-            slot = b * 2 + r
-            sl = idx * SLOTS + slot
-            sp, es = tab[idx, slot], tab[idx, SLOTS + slot]
-            columns = []
-            for h in range(heads):
-                hs = pl.ds(h * HEAD_DIM, HEAD_DIM)
-                vs = pick([kv[1, idx, e, :, hs] for e in range(3)], es)
-                dp = lax.dot_general(g_blk[b][sp, :, hs], vs, (((1,), (1,)), ((), ())),
-                                     preferred_element_type=jnp.float32)
-                dpb[sl, :, hs] = dp
-                columns.append(jnp.sum(pb[sl, :, hs] * dp, axis=1, keepdims=True))
-            insert(gp, idx, slot, columns)
+        item(n, b, grad_slot, g_blk, gp)
 
     def items(work, lo, hi, b):
         lax.fori_loop(lo, hi, lambda n, t: (work(n, b), t)[1], 0)
@@ -242,6 +308,7 @@
         def _():
             for copy in swap:
                 copy.wait_recv()
+            send_far()
 
         lo, hi = done(k - 1), done(k)
         mid = jnp.minimum(lo + 2, hi)
@@ -255,31 +322,31 @@
         pass_on(1, k, 2)
         return t
 
-    both = half - 3
+    both = half - 4
     lax.fori_loop(1, both + 1, gather_step, 0)
     if both < lag:
         for copy in swap:
             copy.wait_recv()
+        send_far()
     own_at = upto(both - 1)
     nbr_at = max((both + 1 - lag) * 4, 0)
-    if half > 2:
+    for k in range(max(half - 3, 1), half - 1):
         for e in range(3):
-            pass_on(0, half - 2, e)
-        pass_on(1, half - 2, 0)
-    items(score_item, own_at, upto(both), 0)
-    items(score_item, nbr_at, upto(both), 1)
+            pass_on(0, k, e)
+    if half > 3:
+        pass_on(1, half - 3, 0)
+    for b in (0, 1):
+        items(score_item, own_at if b == 0 else nbr_at, upto(half - 2), b)
+    take_far()
     for e in range(3):
         pass_on(0, half - 1, e)
-    if half > 2:
-        pass_on(1, half - 2, 1)
-        pass_on(1, half - 2, 2)
+    far_send(0, far_slot(score_slot, far_q))
+    if half > 3:
+        pass_on(1, half - 3, 1)
+        pass_on(1, half - 3, 2)
     for b in (0, 1):
-        items(score_item, upto(both), upto(half - 1), b)
-    for b in (0, 1):
-        items(grad_item, nbr_at, upto(half - 2), b)
-    end_gather(0)
-    for b in (0, 1):
-        items(score_item, upto(half - 1), 2 * half, b)
+        items(score_item, upto(half - 2), upto(half - 1), b)
+    far_insert(0, lse)
 
     def exchange(i, value):
         st_s[i] = value
@@ -297,28 +364,41 @@
     total = top + jnp.log(jnp.exp(lc - top) + jnp.exp(lo_ - top))
     wts[0] = jnp.exp(a0 - total)
     wts[1] = jnp.exp(a1 - total)
-    for e in range(3):
-        pass_on(1, half - 1, e)
-
-    def column(values, lane):
-        return jnp.sum(jnp.where(lanes == lane, values, 0.0), axis=1, keepdims=True)
-
-    def contribution(c, idx, h):
+
+    def slot_lanes(idx, slot, h):
+        return (tab[idx, 2 * SLOTS + slot] + h * stride, tab[idx, 3 * SLOTS + slot] + h * stride)
+
+    def weight(lane0, lane1):
+        w = jnp.where(lanes == lane0, wts[0], 0.0) + jnp.where(lanes == lane1, wts[1], 0.0)
+        return jnp.sum(w, axis=1, keepdims=True)
+
+    far_send(2, lambda b, r: [weight(*slot_lanes(half, b * 2 + r, h)) for h in range(heads)])
+    if half > 2:
+        pass_on(1, half - 2, 0)
+        pass_on(1, half - 2, 1)
+
+    def contribution(c, idx, h, f=None):
         hs = pl.ds(h * HEAD_DIM, HEAD_DIM)
         left, right = [], []
-        for slot in range(SLOTS):
-            b = slot // 2
-            sl = idx * SLOTS + slot
-            sp, es = tab[idx, slot], tab[idx, SLOTS + slot]
-            l0 = tab[idx, 2 * SLOTS + slot] + h * stride
-            l1 = tab[idx, 3 * SLOTS + slot] + h * stride
-            w = jnp.where(lanes == l0, wts[0], 0.0) + jnp.where(lanes == l1, wts[1], 0.0)
-            p = pb[sl, :, hs] * jnp.sum(w, axis=1, keepdims=True)
+        for slot in range(SLOTS) if f is None else range(SLOTS, SLOTS + 2):
+            if slot < SLOTS:
+                sl = idx * SLOTS + slot
+                sp, es = tab[idx, slot], tab[idx, SLOTS + slot]
+                l0, l1 = slot_lanes(idx, slot, h)
+                w = weight(l0, l1)
+                rows = (q_blk, g_blk)[c][slot // 2][sp, :, hs]
+            else:
+                r = slot - SLOTS
+                sl = half * SLOTS + f * 2 + r
+                es = far_entry(f, r)
+                w = far_get(2, f, r, h)
+                rows = (far_q, far_g)[c][1, f, r, :, hs]
+            p = pb[sl, :, hs] * w
             if c == 0:
-                p = p * (dpb[sl, :, hs] - column(dlt[...], jnp.maximum(l0, l1)))
-                right.append(q_blk[b][sp, :, hs])
-            else:
-                right.append(g_blk[b][sp, :, hs])
+                delta = (column(dlt[...], jnp.maximum(l0, l1)) if slot < SLOTS
+                         else far_get(3, f, r, h))
+                p = p * (dpb[sl, :, hs] - delta)
+            right.append(rows)
             x = p.astype(jnp.bfloat16)
             zero = jnp.zeros_like(x)
             left.append(jnp.concatenate([jnp.where(es == e, x, zero) for e in range(3)], axis=1))
@@ -343,17 +423,17 @@
     def contribute_both(c, m):
         lax.fori_loop(0, 2, lambda d, t: (contribute(c, jnp.where(d == 0, m, nz - m), d), t)[1], 0)
 
-    def start_sums(c):
-        contribute(c, half, 0)
-        for e in range(3):
-            d = far(c, e)
-            rs[d, c, half, e] = cbuf[c, 0, e].astype(jnp.bfloat16)
-            step_on(d, c, half, e).start()
-        contribute_both(c, half - 1)
-        for e in range(3):
-            d = 1 - far(c, e)
-            rs[d, c, half - 1, e] = cbuf[c, d, e].astype(jnp.bfloat16)
-            step_on(d, c, half - 1, e).start()
+    def far_contribute(c):
+        for d in (0, 1):
+            for h in range(heads):
+                hs = pl.ds(h * HEAD_DIM, HEAD_DIM)
+                o = cbuf[c, d, :, :, hs] + contribution(c, far_at(d), h, d)
+                rs[d, c, half - 1, :, :, hs] = o.astype(jnp.bfloat16)
+
+    def start_sums(c, entries):
+        for e in entries:
+            for d in (0, 1):
+                step_on(d, c, half - 1, e).start()
 
     def add_on(c, d, m, e):
         sum_arrived(d, c, m, e)
@@ -384,7 +464,9 @@
                 es = tab_u[b * 3 + 2, at]
                 w = column(wts[j], y_b * ch + sp + h * stride)
                 p = (pb[sl, :, hs] * w).astype(jnp.bfloat16)
-                acc += jnp.dot(p, kv[1, idx, es, :, hs], preferred_element_type=jnp.float32)
+                near = jnp.dot(p, kv[1, idx, es, :, hs], preferred_element_type=jnp.float32)
+                away = far_a[1, b, lax.rem(tab_u[b * 3 + 1, at], 2), :, hs].astype(jnp.float32)
+                acc += jnp.where(idx == half, away, near)
             outs.append((hs, acc))
         return outs
 
@@ -402,22 +484,54 @@
     give = remote(asend, arecv, a_s.at[0], a_r.at[0], y_nbr)
     out_copy = pltpu.make_async_copy(att, att_out, o_l.at[0])
 
-    start_sums(1)
-    end_gather(1)
+    contribute_both(1, half - 1)
+    if half > 2:
+        pass_on(1, half - 2, 2)
+    for f in (0, 1):
+        far_tile(2, f).wait_recv()
+    far_contribute(1)
     for b in (0, 1):
-        items(grad_item, upto(half - 2), 2 * half, b)
+        items(grad_item, nbr_at, upto(half - 2), b)
+    start_sums(1, (0,))
+    for e in range(3):
+        pass_on(1, half - 1, e)
+    far_send(1, far_slot(grad_slot, far_g))
+    start_sums(1, (1,))
+    for b in (0, 1):
+        items(grad_item, upto(half - 2), upto(half - 1), b)
+    far_insert(1, gp)
     gc = wts[0] * gp[0] + wts[1] * gp[1]
     stats.append(exchange(1, gc))
     dlt[...] = gc + st_r[1]
-    start_sums(0)
-    for e in range(3):
-        for c in (1, 0):
-            add_on(c, far(c, e), half - 1, e)
+    far_send(3, lambda b, r: [
+        column(dlt[...], jnp.maximum(*slot_lanes(half, b * 2 + r, h))) for h in range(heads)])
+    start_sums(1, (2,))
+    contribute_both(0, half - 1)
+
+    for f in (0, 1):
+        for r in (0, 1):
+            for h in range(heads):
+                hs = pl.ds(h * HEAD_DIM, HEAD_DIM)
+                p = (pb[half * SLOTS + f * 2 + r, :, hs] * far_get(2, f, r, h)).astype(jnp.bfloat16)
+                o = jnp.dot(p, kv[1, far_at(f), far_entry(f, r), :, hs],
+                            preferred_element_type=jnp.float32)
+                far_a[0, f, r, :, hs] = o.astype(jnp.bfloat16)
+    for f in (0, 1):
+        far_tile(3, f).wait_recv()
+    far_contribute(0)
+    start_sums(0, (0, 1, 2))
+    for f in (0, 1):
+        far_part(f).start()
 
     def spans(k):
         if half < 8:
             return
 
+        @pl.when(k == 2)
+        def _():
+            for f in (0, 1):
+                far_part(f).wait_recv()
+
         @pl.when(k <= 3)
         def _():
             lax.fori_loop((k - 2) * (ch // 2), (k - 1) * (ch // 2), nbr_span, 0)
@@ -437,6 +551,26 @@
         @pl.when(k == 7)
         def _():
             out_copy.start()
+
+    def early_sent(c):
+        for d in (0, 1):
+            for e in range(3):
+                first(d, c, e).wait_send()
+                lax.fori_loop(2, half, lambda k, t: (forward(d, c, k, e).wait_send(), t)[1], 0)
+
+    def small_sent():
+        for b in (0, 1):
+            for copy in ([far_spans(0, b), far_spans(1, b), far_table(b), far_part(b)]
+                         + [far_tile(i, b) for i in range(4)]):
+                copy.wait_send()
+        for copy in locals_ + swap + maps + stats + [give]:
+            copy.wait_send()
+
+    def sums_sent(m):
+        for c in (0, 1):
+            for d in (0, 1):
+                for e in range(3):
+                    step_on(d, c, m, e).wait_send()
 
     def sum_step(k, t):
         m = half - k
@@ -447,10 +581,21 @@
                 for d in (0, 1):
                     add_on(c, d, m, e)
         spans(k)
+        if half >= 8:
+            pl.when(k == 4)(lambda: early_sent(0))
+            pl.when(k == 5)(lambda: early_sent(1))
+            pl.when(k == 7)(small_sent)
+
+        @pl.when(k >= 3)
+        def _():
+            sums_sent(m + 2)
+
         return t
 
     lax.fori_loop(2, half, sum_step, 0)
     if half < 8:
+        for f in (0, 1):
+            far_part(f).wait_recv()
         lax.fori_loop(0, ch, nbr_span, 0)
         give.start()
         give.wait_recv()
@@ -462,15 +607,12 @@
         for c in (1, 0):
             last_sum(c, e)
 
-    for c in (0, 1):
-        for d in (0, 1):
-            for e in range(3):
-                first(d, c, e).wait_send()
-                steps = half + 1 if far(c, e) == d else half
-                lax.fori_loop(2, steps, lambda k, t: (forward(d, c, k, e).wait_send(), t)[1], 0)
-                lax.fori_loop(1, steps, lambda m, t: (step_on(d, c, m, e).wait_send(), t)[1], 0)
-    for copy in locals_ + swap + maps + stats + [give]:
-        copy.wait_send()
+    if half < 8:
+        early_sent(0)
+        early_sent(1)
+        small_sent()
+    for m in sorted({1, min(2, half - 1)}):
+        sums_sent(m)
     for c in (0, 1):
         for e in range(3):
             give_back(c, e).wait_send()
@@ -515,6 +657,10 @@
             pltpu.VMEM((2, nt, 8, 128), jnp.int32), pltpu.VMEM((nz, 128), jnp.int32),
             pltpu.VMEM((8, 128), jnp.int32), pltpu.SMEM((nz, 128), jnp.int32),
             pltpu.SMEM((8, 128), jnp.int32), dma((2, nt)), dma((2, nt)), dma((2,)),
+            pltpu.VMEM((2, 2, 2, SPAN, width), bf), pltpu.VMEM((2, 2, 2, SPAN, width), bf),
+            pltpu.VMEM((2, nz, 128), jnp.int32), pltpu.SMEM((2, nz, 128), jnp.int32),
+            pltpu.VMEM((2, 4, 2, SPAN, 128), f32), pltpu.VMEM((2, 2, 2, SPAN, width), bf),
+            dma((8, 2)), dma((8, 2)), dma((2,)),
         ],
         compiler_params=pltpu.CompilerParams(
             collective_id=0, has_side_effects=True, vmem_limit_bytes=60 * 1024 * 1024),

time: 281 us -> 279 us (level)
  no operation moved by 1% of the time
where the time goes in v4:
time: 279 us
  Pallas kernels  275 us (99%)
  local copies, waits for them, and re-layouts  3.22 us (1%)
    pallas_call x1, Pallas kernels, per_device(): pl.pallas_call(functools.partial(kernel, nz, nt, ch, heads), out_shape=[j...  275 us

profile of v4, /device:TPU:1, one launch (start us, length us, event | category | flops | bytes accessed | tf_op | source)
XLA Modules:
  0.0 278.5 jit_solution(10050006530442553186)
XLA Ops:
  0.6 274.6 %shard_map.77 = (bf16[16,64,512]{2,1,0:T(8,128)(2,1)}, bf16[2,3,128,512]{3,2,1,0:T(8,128)(2,1)}) custom-call(s32[2,2]{1,0:T(2,128)} %owner_in.1, s32[2,2]{1,0:T(2,128)} %entry_in.1, s32[2]{0:T(128)} %count_in.1, bf16[16,64,512]{2,1,0:T(8,128)(2,1)} %bitcast.7, bf16[2,3,128,512]{3,2,1,0:T(8,128)(2,1)} %bitcast.9, bf16[16,64,512]{2,1,0:T(8,128)(2,1)} %bitcast.8), custom_call_target="tpu_custom_call" | custom-call | flops 4000000000 | bytes 6000000 | tf_op jit(solution)/shard_map/pallas_call | solution.py:635
  275.3 0.0 copy-start
  275.3 2.3 copy.10
  277.6 0.0 copy-done
  277.6 0.9 copy.11
Async XLA Ops:
  275.3 2.3 copy-start

commit v5 on v4

--- a/solution.py
+++ b/solution.py
@@ -15,6 +15,7 @@
 MESH = pl.DeviceIdType.MESH
 DEAD = -1e30
 NONE = -100000
+PIECES = 4
 
 
 def kernel(nz, nt, ch, heads, owner_in, entry_in, count_in, q_in, kv_in, g_in, att_out, sg_out,
@@ -497,6 +498,10 @@
         pass_on(1, half - 1, e)
     far_send(1, far_slot(grad_slot, far_g))
     start_sums(1, (1,))
+    if half > 2:
+        contribute_both(1, half - 2)
+        for d in (0, 1):
+            add_on(1, d, half - 2, 0)
     for b in (0, 1):
         items(grad_item, upto(half - 2), upto(half - 1), b)
     far_insert(1, gp)
@@ -574,12 +579,19 @@
 
     def sum_step(k, t):
         m = half - k
-        contribute_both(1, m)
+        pl.when(k > 2)(lambda: contribute_both(1, m))
         contribute_both(0, m)
+
+        @pl.when(k > 2)
+        def _():
+            for d in (0, 1):
+                add_on(1, d, m, 0)
+
         for e in range(3):
             for c in (1, 0):
-                for d in (0, 1):
-                    add_on(c, d, m, e)
+                if c == 0 or e > 0:
+                    for d in (0, 1):
+                        add_on(c, d, m, e)
         spans(k)
         if half >= 8:
             pl.when(k == 4)(lambda: early_sent(0))
@@ -618,6 +630,22 @@
             give_back(c, e).wait_send()
             give_back(c, e).wait_recv()
     out_copy.wait()
+
+
+def place_results(att_in, sums_in, att_out, sums_out, att, sums, in_sem, out_sem):
+    size = att_in.shape[0] // PIECES
+    parts = [[ref.at[pl.ds(i * size, size)] for ref in (att_in, att, att_out)]
+             for i in range(PIECES)]
+    parts += [[ref.at[c] for ref in (sums_in, sums, sums_out)] for c in range(2)]
+    loads = [pltpu.make_async_copy(a, b, in_sem.at[i]) for i, (a, b, _) in enumerate(parts)]
+    stores = [pltpu.make_async_copy(b, c, out_sem.at[i]) for i, (_, b, c) in enumerate(parts)]
+    for copy in loads:
+        copy.start()
+    for load, store in zip(loads, stores):
+        load.wait()
+        store.start()
+    for copy in stores:
+        copy.wait()
 
 
 def per_device(nz, queries, store_kv, out_grad, neighbour_owner, neighbour_slot, neighbour_count):
@@ -667,6 +695,15 @@
         cost_estimate=pl.CostEstimate(flops=4 * 10 ** 9, bytes_accessed=6 * 10 ** 6,
                                       transcendentals=4 * 10 ** 6),
     )(neighbour_owner, neighbour_slot, neighbour_count, queries.reshape(spans), store_kv.reshape((2,) + block), out_grad.reshape(spans))
+    attended, store_grad = pl.pallas_call(
+        place_results,
+        out_shape=[jax.ShapeDtypeStruct(spans, bf), jax.ShapeDtypeStruct((2,) + block, bf)],
+        in_specs=[any_spec, any_spec],
+        out_specs=[any_spec, any_spec],
+        scratch_shapes=[pltpu.VMEM(spans, bf), pltpu.VMEM((2,) + block, bf),
+                        dma((PIECES + 2,)), dma((PIECES + 2,))],
+        compiler_params=pltpu.CompilerParams(vmem_limit_bytes=60 * 1024 * 1024),
+    )(attended, store_grad)
     return attended.reshape(rows, width), store_grad.reshape(store_kv.shape)
 
 

time: 279 us -> 276 us (0.989)
  local copies, waits for them, and re-layouts: 3.22 us -> 0 us
    unnamed x4 -> x0, local copies, waits for them, and re-layouts: 3.22 us -> none
where the time goes in v5:
time: 276 us
  Pallas kernels  275 us (100%)
    pallas_call x1, Pallas kernels, per_device(): pl.pallas_call(functools.partial(kernel, nz, nt, ch, heads), out_shape=[j...  273 us

profile of v5, /device:TPU:1, one launch (start us, length us, event | category | flops | bytes accessed | tf_op | source)
XLA Modules:
  0.0 276.0 jit_solution(771889951802954229)
XLA Ops:
  0.6 272.9 %shard_map.77 = (bf16[16,64,512]{2,1,0:T(8,128)(2,1)}, bf16[2,3,128,512]{3,2,1,0:T(8,128)(2,1)}) custom-call(s32[2,2]{1,0:T(2,128)} %owner_in.1, s32[2,2]{1,0:T(2,128)} %entry_in.1, s32[2]{0:T(128)} %count_in.1, bf16[16,64,512]{2,1,0:T(8,128)(2,1)} %bitcast.5, bf16[2,3,128,512]{3,2,1,0:T(8,128)(2,1)} %bitcast.8, bf16[16,64,512]{2,1,0:T(8,128)(2,1)} %bitcast.6), custom_call_target="tpu_custom_call" | custom-call | flops 4000000000 | bytes 6000000 | tf_op jit(solution)/shard_map/pallas_call | solution.py:663
  273.5 2.3 shard_map.78

commit v6 on v5

--- a/solution.py
+++ b/solution.py
@@ -491,9 +491,9 @@
     for f in (0, 1):
         far_tile(2, f).wait_recv()
     far_contribute(1)
+    start_sums(1, (0,))
     for b in (0, 1):
         items(grad_item, nbr_at, upto(half - 2), b)
-    start_sums(1, (0,))
     for e in range(3):
         pass_on(1, half - 1, e)
     far_send(1, far_slot(grad_slot, far_g))

time: 276 us -> 275 us (level)
  no operation moved by 1% of the time
where the time goes in v6:
time: 275 us
  Pallas kernels  274 us (100%)
    pallas_call x1, Pallas kernels, per_device(): pl.pallas_call(functools.partial(kernel, nz, nt, ch, heads), out_shape=[j...  272 us

profile of v6, /device:TPU:1, one launch (start us, length us, event | category | flops | bytes accessed | tf_op | source)
XLA Modules:
  0.0 275.0 jit_solution(11613509136325152151)
XLA Ops:
  0.6 271.9 %shard_map.77 = (bf16[16,64,512]{2,1,0:T(8,128)(2,1)}, bf16[2,3,128,512]{3,2,1,0:T(8,128)(2,1)}) custom-call(s32[2,2]{1,0:T(2,128)} %owner_in.1, s32[2,2]{1,0:T(2,128)} %entry_in.1, s32[2]{0:T(128)} %count_in.1, bf16[16,64,512]{2,1,0:T(8,128)(2,1)} %bitcast.5, bf16[2,3,128,512]{3,2,1,0:T(8,128)(2,1)} %bitcast.8, bf16[16,64,512]{2,1,0:T(8,128)(2,1)} %bitcast.6), custom_call_target="tpu_custom_call" | custom-call | flops 4000000000 | bytes 6000000 | tf_op jit(solution)/shard_map/pallas_call | solution.py:663
  272.5 2.3 shard_map.78
